TPU v7x, 512 devices: a whole 4x4x16 slice. The times are simulated.
512 devices in a mesh: tube: 16 (over z), lon: 32 (over y, x, core).
Axes of the slice: x: 4, y: 4, z: 16, core: 2. Of those that a mesh axis runs over, the one named last changes fastest.
Arguments:
- density: float32 [7, 512, 256, 128], P(None, 'tube', 'lon'), may hold values from 0.5 to 5
- pedersen: float32 [512, 256, 128], P('tube', 'lon'), may hold values from 0.1 to 10
- neutral_wind: float32 [512, 256, 128], P('tube', 'lon'), may hold values from -6 to 6
- along_courant: float32 [7, 512], P(None, 'tube'), may hold values from 0.45 to 20000
Outputs:
- density_next: float32 [7, 512, 256, 128], P(None, 'tube', 'lon')
- potential: float32 [256, 128], P('lon')
All inputs are finite; a program needn't handle non-finite values.
Results may differ from a plain program's by a relative error of at most 0.00016.
Values sent between devices are 32-bit elements; how exact they have to be, the bound alone decides.
A program may use at most 64 MiB of HBM per device.

v0:
```python
import functools

import jax
import jax.numpy as jnp
from jax import lax
from jax.experimental import pallas as pl
from jax.experimental.pallas import tpu as pltpu
from jax.sharding import PartitionSpec as P

F32 = jnp.float32
SCREENING = 0.005
CAP = 0.2
NV = 32
CYCLES = 3
MESH = pl.DeviceIdType.MESH


def exchange_kernel(
    nt, nl, ped, wind, cour, dens, gath, halo, ent, ent_l, ent_r,
    part, recv1, row, recv2, dloc, atab, btab, bsend, brecv, psend,
    s_ld, s_rs, r_rs, s_ag, r_ag, s_lg, r_lg, s_h, r_h, s_b, r_b, s_p, r_p, s_e, r_e,
):
    ns, pts = dens.shape[0], dens.shape[1]
    rp = 16 // nt
    t, l = lax.axis_index("tube"), lax.axis_index("lon")

    load = pltpu.make_async_copy(dens, dloc, s_ld)
    load.start()

    barrier = pltpu.get_barrier_semaphore()
    for o in range(1, nt):
        pl.semaphore_signal(
            barrier, inc=1, device_id=(lax.rem(t + o, nt), l), device_id_type=MESH
        )
    for o in range(1, nl):
        pl.semaphore_signal(
            barrier, inc=1, device_id=(t, lax.rem(l + o, nl)), device_id_type=MESH
        )

    csum = [ped[k] for k in range(4)]
    ssum = [ped[k] * wind[k] for k in range(4)]
    for p in range(4, pts):
        csum[p % 4] = csum[p % 4] + ped[p]
        ssum[p % 4] = ssum[p % 4] + ped[p] * wind[p]
    csum = (csum[0] + csum[1]) + (csum[2] + csum[3])
    ssum = (ssum[0] + ssum[1]) + (ssum[2] + ssum[3])
    for r in range(8):
        part[r // rp, r % rp, :] = csum[r]
        part[(8 + r) // rp, r % rp, :] = ssum[r]

    pl.semaphore_wait(barrier, nt + nl - 2)

    def remote(src, dst, ssem, rsem, to):
        c = pltpu.make_async_remote_copy(
            src_ref=src, dst_ref=dst, send_sem=ssem, recv_sem=rsem,
            device_id=to, device_id_type=MESH,
        )
        c.start()
        return c

    rs = []
    for o in range(1, nt):
        to = lax.rem(t + o, nt)
        rs.append(remote(part.at[to], recv1.at[o], s_rs.at[o], r_rs.at[o], (to, l)))
    recv1[0] = part[t]

    right, left = lax.rem(l + 1, nl), lax.rem(l + nl - 1, nl)
    h0 = remote(
        dens.at[:, :, pl.ds(7, 1), :], halo.at[:, :, pl.ds(0, 1), :], s_h.at[0], r_h.at[0], (t, right)
    )
    h1 = remote(
        dens.at[:, :, pl.ds(0, 1), :], halo.at[:, :, pl.ds(7, 1), :], s_h.at[1], r_h.at[1], (t, left)
    )

    coefficient_tables(cour, atab, btab)
    load.wait()

    def step(p, carry):
        out = []
        for s in range(ns):
            x, m = carry[s]
            a, b = row_of(atab, p * 8 + s), row_of(btab, p * 8 + s)
            out.append((a * x + b * dloc[s, p], a * m))
        return tuple(out)

    zero, one = jnp.zeros((8, 128), F32), jnp.ones((8, 128), F32)
    ends = lax.fori_loop(0, pts, step, tuple((zero, one) for _ in range(ns)))
    for s in range(ns):
        bsend[s, 0] = ends[s][0]
        bsend[s, 1] = ends[s][1]

    for c in rs:
        c.wait_recv()
    total = recv1[0]
    for o in range(1, nt):
        total = total + recv1[o]
    row[...] = total
    ag = []
    for o in range(1, nt):
        to = lax.rem(t + o, nt)
        ag.append(remote(row, recv2.at[t], s_ag.at[o], r_ag.at[o], (to, l)))
    recv2[t] = total

    mine = (t * ns + nt - 1) // nt
    owner_of = [(s * nt) // ns for s in range(ns)]
    is_owner = jnp.logical_and(mine < ns, (mine * nt) // ns == t)
    for s in range(ns):

        @pl.when(t != owner_of[s])
        def _():
            o = lax.rem(t - owner_of[s] + nt, nt)
            remote(bsend.at[s], brecv.at[o], s_b.at[s], r_b.at[o], (owner_of[s], l))

    for c in ag:
        c.wait_recv()
    own = pltpu.make_async_copy(recv2, gath.at[l], s_lg.at[0])
    own.start()
    lg = []
    for o in range(1, nl):
        to = lax.rem(l + o, nl)
        lg.append(remote(recv2, gath.at[l], s_lg.at[o], r_lg.at[o], (t, to)))

    @pl.when(is_owner)
    def _():
        brecv[0] = bsend[mine]
        for o in range(1, nt):
            pltpu.make_async_copy(brecv.at[o], brecv.at[o], r_b.at[o]).wait()
        x = zero
        for k in range(nt):
            psend[k] = x
            o = lax.rem(k - t + nt, nt)
            x = brecv[o, 1] * x + brecv[o, 0]
        ent[mine] = psend[t]
        for o in range(1, nt):
            to = lax.rem(t + o, nt)
            remote(psend.at[to], ent.at[mine], s_p.at[o], r_p.at[mine], (to, l))

    for s in range(ns):

        @pl.when(t != owner_of[s])
        def _():
            pltpu.make_async_copy(ent.at[s], ent.at[s], r_p.at[s]).wait()

    e0 = remote(ent, ent_l, s_e.at[0], r_e.at[0], (t, right))
    e1 = remote(ent, ent_r, s_e.at[1], r_e.at[1], (t, left))

    own.wait()
    for c in rs + ag + lg:
        c.wait_send()
    for c in lg:
        c.wait_recv()
    for s in range(ns):

        @pl.when(t != owner_of[s])
        def _():
            pltpu.make_async_copy(bsend.at[s], bsend.at[s], s_b.at[s]).wait()

    @pl.when(is_owner)
    def _():
        for o in range(1, nt):
            pltpu.make_async_copy(psend.at[0], psend.at[0], s_p.at[o]).wait()

    for c in (h0, h1, e0, e1):
        c.wait()


def exchange(mesh, density, pedersen, wind, courant):
    nt, nl = mesh.shape["tube"], mesh.shape["lon"]
    ns, pts = density.shape[:2]
    rp = 16 // nt
    vm = pl.BlockSpec(memory_space=pltpu.VMEM)
    hbm = pl.BlockSpec(memory_space=pl.ANY)
    dma = pltpu.SemaphoreType.DMA
    state = jax.ShapeDtypeStruct((ns, 8, 128), F32)
    return pl.pallas_call(
        functools.partial(exchange_kernel, nt, nl),
        out_shape=(
            jax.ShapeDtypeStruct((nl, nt, rp, 128), F32),
            jax.ShapeDtypeStruct(density.shape, F32),
            state, state, state,
        ),
        in_specs=[vm, vm, vm, hbm],
        out_specs=(vm, hbm, vm, vm, vm),
        scratch_shapes=[
            pltpu.VMEM((nt, rp, 128), F32),
            pltpu.VMEM((nt, rp, 128), F32),
            pltpu.VMEM((rp, 128), F32),
            pltpu.VMEM((nt, rp, 128), F32),
            pltpu.VMEM(density.shape, F32),
            pltpu.VMEM((pts * 8, 128), F32),
            pltpu.VMEM((pts * 8, 128), F32),
            pltpu.VMEM((ns, 2, 8, 128), F32),
            pltpu.VMEM((nt, 2, 8, 128), F32),
            pltpu.VMEM((nt, 8, 128), F32),
            dma,
            dma((nt,)), dma((nt,)), dma((nt,)), dma((nt,)),
            dma((nl,)), dma((nl,)),
            dma((2,)), dma((2,)),
            dma((ns,)), dma((nt,)),
            dma((nt,)), dma((ns,)),
            dma((2,)), dma((2,)),
        ],
        compiler_params=pltpu.CompilerParams(
            collective_id=0, has_side_effects=True, vmem_limit_bytes=40 * 2**20
        ),
        name="exchange",
    )(pedersen, wind, courant, density)


def row_of(ref, r):
    return jnp.broadcast_to(ref[pl.ds(r, 1), :], (8, 128))


def coefficient_tables(cour, atab, btab):
    c = cour[...]
    inv = 1.0 / (1.0 + c)
    keep = c * inv
    ns, pts = c.shape
    for p in range(pts):
        atab[pl.ds(p * 8, ns), :] = jnp.broadcast_to(keep[:, p : p + 1], (ns, 128))
        btab[pl.ds(p * 8, ns), :] = jnp.broadcast_to(inv[:, p : p + 1], (ns, 128))


def lroll(x, shift):
    return pltpu.roll(x, shift % 128, x.ndim - 1)


def before(x):
    return [pltpu.roll(x[-1], 1, 0)] + x[:-1]


def after(x):
    return x[1:] + [pltpu.roll(x[0], 7, 0)]


def level_weights(cond, level, wl, ws, wn, kk, dd):
    half, step, n = 0.5 * 0.25**level, 2**level, len(cond)
    lane = lax.broadcasted_iota(jnp.int32, (8, 128), 1)
    lo, hi = lane >= step, lane < 128 - step
    west = [half * (a + b) for a, b in zip(before(cond), cond)]
    west.append(pltpu.roll(west[0], 7, 0))
    for v in range(n + 1):
        wl[v] = west[v]
    for v in range(n):
        c = cond[v]
        south = half * (c + jnp.where(lo, lroll(c, step), 0.0))
        north = half * (c + jnp.where(hi, lroll(c, -step), 0.0))
        ws[v] = jnp.where(lo, south, 0.0)
        wn[v] = jnp.where(hi, north, 0.0)
        diagonal = (west[v] + west[v + 1]) + (south + north) + SCREENING
        kk[v] = 0.8 / diagonal
        if dd is not None:
            dd[v] = diagonal


def coarsened(x, step):
    lane = lax.broadcasted_iota(jnp.int32, (8, 128), 1)
    low = (lane // step) % 2 == 0
    out = []
    for v in range(0, len(x), 2):
        y = x[v] + x[v + 1]
        out.append(0.25 * (y + jnp.where(low, lroll(y, -step), lroll(y, step))))
    return out


def pulled(x, w, level):
    wl, ws, wn = w[:3]
    step, b, a = 2**level, before(x), after(x)
    return [
        (wl[v] * b[v] + wl[v + 1] * a[v])
        + (ws[v] * lroll(x[v], step) + wn[v] * lroll(x[v], -step))
        for v in range(len(x))
    ]


def vcycle(level, rhs, start, w, coarse):
    if level == len(w):
        return coarse(rhs)
    n = len(rhs)
    kk = w[level][3]
    if start is None:
        x = [kk[v] * rhs[v] for v in range(n)]
        e = [0.2 * r + p for r, p in zip(rhs, pulled(x, w[level], level))]
    else:
        dd = w[level][4]
        p = pulled(start, w[level], level)
        x = [0.2 * start[v] + kk[v] * (rhs[v] + p[v]) for v in range(n)]
        p = pulled(x, w[level], level)
        e = [(rhs[v] - dd[v] * x[v]) + p[v] for v in range(n)]
    fix = vcycle(level + 1, coarsened(e, 2**level), None, w, coarse)
    x = [x[v] + fix[v // 2] for v in range(n)]
    p = pulled(x, w[level], level)
    return [0.2 * x[v] + kk[v] * (rhs[v] + p[v]) for v in range(n)]


def to_ring(x, sq, sq2):
    for v in range(4):
        for rep in range(4):
            sq[pl.ds(rep * 32 + v, 8, stride=4), :] = x[v]
    sq2[...] = sq[...].T
    return [sq2[pl.ds(0, 8, stride=8), :], sq2[pl.ds(64, 8, stride=8), :]]


def from_ring(x, sq, sq2, vec):
    vec[pl.ds(0, 8), :], vec[pl.ds(8, 8), :] = x[0], x[1]
    for j in range(16):
        sq[pl.ds(j * 8, 8), :] = row_of(vec, j)
    sq2[...] = sq[...].T
    return [sq2[pl.ds(v, 8, stride=4), :] for v in range(4)]


def ring_matrix(c, bmat, emat):
    sub = [lax.broadcasted_iota(jnp.int32, (8, 128), 0) + 8 * h for h in range(2)]
    half = 0.5 * 0.25**3
    east = [half * (c[h] + lroll(c[h], -1)) for h in range(2)]
    up = [pltpu.roll(c[h], 1, 0) for h in range(2)]
    dn = [pltpu.roll(c[h], 7, 0) for h in range(2)]
    first, last = sub[0] % 8 == 0, sub[0] % 8 == 7
    below = [jnp.where(first, 0.0, up[0]), jnp.where(first, up[0], up[1])]
    above = [jnp.where(last, dn[1], dn[0]), jnp.where(last, 0.0, dn[1])]
    south = [half * (c[h] + below[h]) for h in range(2)]
    north = [half * (c[h] + above[h]) for h in range(2)]
    for i in range(16):
        for h in range(2):
            j = sub[h]
            diagonal = (east[h] + lroll(east[h], 1)) + (south[h] + north[h]) + SCREENING
            value = jnp.where(j == i, diagonal, 0.0)
            value = jnp.where(j == i + 1, -south[h], value)
            value = jnp.where(j == i - 1, -north[h], value)
            bmat[pl.ds(i * 16 + h * 8, 8), :] = value
            emat[pl.ds(i * 16 + h * 8, 8), :] = jnp.where(j == i, -east[h], 0.0)


def mat(ref, i, h, base=0):
    return ref[pl.ds(base + i * 16 + h * 8, 8), :]


def matT(ref, i, h, base=0):
    return ref[pl.ds(base + h * 128 + i, 8, stride=16), :]


def inverted(a, pivots):
    sub = [lax.broadcasted_iota(jnp.int32, (8, 128), 0) + 8 * h for h in range(2)]
    for k in range(16):
        hk = k // 8
        base = k * 16
        for h in range(2):
            pivots[pl.ds(base + h * 8, 8), :] = a[k][h]
        p = 1.0 / row_of(pivots, base + k)
        scaled = [a[k][h] * p for h in range(2)]
        rk = list(scaled)
        rk[hk] = jnp.where(sub[hk] == k, 1.0 + p, rk[hk])
        new = []
        for i in range(16):
            if i == k:
                fin = list(scaled)
                fin[hk] = jnp.where(sub[hk] == k, p, fin[hk])
                new.append(fin)
                continue
            f = row_of(pivots, base + i)
            if i < k:
                f = -f
            new.append([a[i][h] - f * rk[h] for h in range(2)])
        a = new
    return a


def put(ref, a, base=0):
    for i in range(16):
        for h in range(2):
            ref[pl.ds(base + i * 16 + h * 8, 8), :] = a[i][h]


def product(left, rights):
    outs = [[] for _ in rights]
    for i in range(16):
        acc = [[None, None] for _ in rights]
        for k in range(16):
            f = row_of(left, i * 16 + k)
            for q, right in enumerate(rights):
                for h in range(2):
                    term = f * right[k][h]
                    acc[q][h] = term if k == 0 else acc[q][h] + term
        for q in range(len(rights)):
            outs[q].append(acc[q])
    return outs


def factor(bmat, emat, gs, xs, xts, left, pivots):
    lane = lax.broadcasted_iota(jnp.int32, (8, 128), 1)
    both = [(i, h) for i in range(16) for h in range(2)]

    def body(m, _):
        d = jnp.left_shift(1, m)
        odd = jnp.bitwise_and(lane, d) != 0
        base = pl.multiple_of(m * 256, 256)
        g = inverted([[mat(bmat, i, h) for h in range(2)] for i in range(16)], pivots)
        put(gs, g, base)

        def ahead(x):
            return pltpu.roll(x, 128 - d, 1)

        for i, h in both:
            left[pl.ds(i * 16 + h * 8, 8), :] = jnp.where(odd, g[i][h], ahead(g[i][h]))
        f = [
            [jnp.where(odd, mat(emat, i, h), matT(emat, i, h)) for h in range(2)] for i in range(16)
        ]
        (x,) = product(left, [f])
        put(xs, x, base)
        for i, h in both:
            xts[pl.ds(base + i * 16 + h * 8, 8), :] = xs[pl.ds(base + h * 128 + i, 8, stride=16), :]
        for i, h in both:
            left[pl.ds(i * 16 + h * 8, 8), :] = jnp.where(odd, matT(emat, i, h), mat(emat, i, h))
        y, n = product(left, [x, [[ahead(x[i][h]) for h in range(2)] for i in range(16)]])
        even = jnp.bitwise_and(lane, 2 * d - 1) == 0
        for i, h in both:
            old = mat(bmat, i, h)
            fresh = old - (y[i][h] + pltpu.roll(y[i][h], d, 1))
            bmat[pl.ds(i * 16 + h * 8, 8), :] = jnp.where(even, fresh, old)
            emat[pl.ds(i * 16 + h * 8, 8), :] = -n[i][h]
        return 0

    lax.fori_loop(0, 5, body, 0)
    last = [
        [mat(bmat, i, h) + (mat(emat, i, h) + matT(emat, i, h)) for h in range(2)] for i in range(16)
    ]
    even = jnp.bitwise_and(lane, 31) == 0
    last = [
        [jnp.where(even, last[i][h], mat(bmat, i, h)) for h in range(2)] for i in range(16)
    ]
    put(gs, inverted(last, pivots), 5 * 256)


def times(ref, base, vec, x):
    vec[pl.ds(0, 8), :], vec[pl.ds(8, 8), :] = x[0], x[1]
    out = []
    for h in range(2):
        terms = [mat(ref, k, h, base) * row_of(vec, k) for k in range(16)]
        while len(terms) > 1:
            terms = [terms[q] + terms[q + 1] for q in range(0, len(terms), 2)]
        out.append(terms[0])
    return out


def ring_solve(r, gs, xs, xts, vecs):
    lane = lax.broadcasted_iota(jnp.int32, (8, 128), 1)
    two = range(2)
    for m in range(5):
        d = 1 << m
        odd, even = (lane & d) != 0, (lane & (2 * d - 1)) == 0
        sel = [jnp.where(odd, r[h], lroll(r[h], -d)) for h in two]
        z = times(xs, m * 256, vecs.at[m], sel)
        r = [jnp.where(even, r[h] - (z[h] + lroll(z[h], d)), r[h]) for h in two]
    x = times(gs, 5 * 256, vecs.at[5], r)
    for m in reversed(range(5)):
        d = 1 << m
        odd, now = (lane & d) != 0, (lane & (2 * d - 1)) == d
        sel = [jnp.where(odd, lroll(x[h], -d), x[h]) for h in two]
        g = times(gs, m * 256, vecs.at[6 + m], r)
        q = times(xts, m * 256, vecs.at[11 + m], sel)
        x = [jnp.where(now, g[h] - (q[h] + lroll(q[h], d)), x[h]) for h in two]
    return x


def potential_of(gath, w, sq, sq2, bmat, emat, gs, xs, xts, left, pivots, vecs):
    scale = 1.0 / 512.0
    at = [pl.ds((v // 8) * 16 + v % 8, 8, stride=64) for v in range(NV)]
    cond = [gath[s, :] * scale for s in at]
    level_weights(cond, 0, *w[0])
    c = coarsened(cond, 1)
    level_weights(c, 1, *w[1])
    c = coarsened(c, 2)
    level_weights(c, 2, *w[2])
    c = coarsened(c, 4)
    ring_matrix(to_ring(c, sq, sq2), bmat, emat)
    factor(bmat, emat, gs, xs, xts, left, pivots)
    at = [pl.ds((v // 8) * 16 + 8 + v % 8, 8, stride=64) for v in range(NV)]
    source = [gath[s, :] * scale for s in at]

    def coarse(r):
        x = ring_solve(to_ring(r, sq, sq2), gs, xs, xts, vecs)
        return from_ring(x, sq, sq2, vecs.at[16])

    x = None
    for _ in range(CYCLES):
        x = vcycle(0, source, x, w, coarse)
    return x


def stencil(pot, west, east):
    lane = lax.broadcasted_iota(jnp.int32, (8, 128), 1)
    low, high = lane == 0, lane == 127

    def slope(q):
        return jnp.where(high, 0.0, lroll(q, -1)) - jnp.where(low, 0.0, lroll(q, 1))

    uw = CAP * jnp.tanh(-0.25 * slope(west + pot))
    ue = CAP * jnp.tanh(-0.25 * slope(pot + east))
    r = east - west
    us = jnp.where(low, 0.0, CAP * jnp.tanh(0.25 * (lroll(r, 1) + r)))
    un = jnp.where(high, 0.0, lroll(us, -1))
    pos = [jnp.maximum(u, 0.0) for u in (uw, ue, us, un)]
    neg = [jnp.minimum(u, 0.0) for u in (uw, ue, us, un)]
    centre = 1.0 - (pos[1] - neg[0]) - (pos[3] - neg[2])
    return centre, pos[0], -neg[1], pos[2], -neg[3]


def solve_kernel(
    gath, ent, ent_l, ent_r, cour, dens_hbm, halo_hbm, out, pot,
    wl0, ws0, wn0, kk0, dd0, wl1, ws1, wn1, kk1, wl2, ws2, wn2, kk2,
    sq, sq2, bmat, emat, gs, xs, xts, left, pivots, vecs, whole, atab, btab, dens, halo, sem,
):
    ns, pts = out.shape[:2]
    l = lax.axis_index("lon")
    loads = [
        pltpu.make_async_copy(dens_hbm, dens, sem.at[0]),
        pltpu.make_async_copy(halo_hbm, halo, sem.at[1]),
    ]
    for c in loads:
        c.start()
    coefficient_tables(cour, atab, btab)
    w = [(wl0, ws0, wn0, kk0, dd0), (wl1, ws1, wn1, kk1, None), (wl2, ws2, wn2, kk2, None)]
    x = potential_of(gath, w, sq, sq2, bmat, emat, gs, xs, xts, left, pivots, vecs)
    for v in range(NV):
        whole[pl.ds(v, 8, stride=NV), :] = x[v]
    own = whole[pl.ds(pl.multiple_of(l * 8, 8), 8), :]
    sub = lax.broadcasted_iota(jnp.int32, (8, 128), 0)
    west = jnp.where(sub == 0, row_of(whole, lax.rem(l * 8 + 255, 256)), pltpu.roll(own, 1, 0))
    east = jnp.where(sub == 7, row_of(whole, lax.rem(l * 8 + 8, 256)), pltpu.roll(own, 7, 0))
    pot[...] = own
    cc, cw, ce, cs, cn = stencil(own, west, east)
    for c in loads:
        c.wait()

    start = []
    for s in range(ns):
        side = jnp.where(sub == 0, pltpu.roll(ent_l[s], 1, 0), pltpu.roll(ent_r[s], 7, 0))
        start.append((ent[s], side))

    def step(p, carry):
        new = []
        for s in range(ns):
            y, side = carry[s]
            a, b = row_of(atab, p * 8 + s), row_of(btab, p * 8 + s)
            y = a * y + b * dens[s, p]
            side = a * side + b * halo[s, p]
            yw = jnp.where(sub == 0, side, pltpu.roll(y, 1, 0))
            ye = jnp.where(sub == 7, side, pltpu.roll(y, 7, 0))
            out[s, p] = (cc * y + (cw * yw + ce * ye)) + (cs * lroll(y, 1) + cn * lroll(y, -1))
            new.append((y, side))
        return tuple(new)

    lax.fori_loop(0, pts, step, tuple(start))


def solve(gath, ent, ent_l, ent_r, courant, density, halo):
    ns, pts = density.shape[:2]
    vm = pl.BlockSpec(memory_space=pltpu.VMEM)
    hbm = pl.BlockSpec(memory_space=pl.ANY)

    def tiles(n):
        return pltpu.VMEM((n, 8, 128), F32)

    def rows(n):
        return pltpu.VMEM((n, 128), F32)

    levels = [tiles(33)] + [tiles(32)] * 4 + [tiles(17)] + [tiles(16)] * 3 + [tiles(9)] + [tiles(8)] * 3
    return pl.pallas_call(
        solve_kernel,
        out_shape=(
            jax.ShapeDtypeStruct(density.shape, F32),
            jax.ShapeDtypeStruct((8, 128), F32),
        ),
        in_specs=[vm] * 5 + [hbm] * 2,
        out_specs=(vm, vm),
        scratch_shapes=levels
        + [rows(128), rows(128), rows(256), rows(256), rows(6 * 256), rows(5 * 256), rows(5 * 256)]
        + [rows(256), rows(256), pltpu.VMEM((17, 16, 128), F32), rows(256)]
        + [rows(pts * 8), rows(pts * 8)]
        + [pltpu.VMEM(density.shape, F32), pltpu.VMEM(density.shape, F32)]
        + [pltpu.SemaphoreType.DMA((2,))],
        compiler_params=pltpu.CompilerParams(vmem_limit_bytes=40 * 2**20),
        name="solve",
    )(gath, ent, ent_l, ent_r, courant, density, halo)


def solution(mesh):
    def on_device(density, pedersen, wind, courant):
        gath, halo, ent, ent_l, ent_r = exchange(mesh, density, pedersen, wind, courant)
        return solve(gath.reshape(-1, 128), ent, ent_l, ent_r, courant, density, halo)

    return jax.shard_map(
        on_device,
        mesh=mesh,
        in_specs=(
            P(None, "tube", "lon", None),
            P("tube", "lon", None),
            P("tube", "lon", None),
            P(None, "tube"),
        ),
        out_specs=(P(None, "tube", "lon", None), P("lon", None)),
        check_vma=False,
    )
```

profile of v0, /device:TPU:1, one launch (start us, length us, event | category | flops | bytes accessed | tf_op | source)
XLA Modules:
  0.0 62.7 jit_solution(14356814011409217418)
XLA Ops:
  0.6 0.0 copy-start
  0.6 1.2 %copy-done = f32[7,32,8,128]{3,2,1,0:T(8,128)S(1)} copy-done((f32[7,32,8,128]{3,2,1,0:T(8,128)S(1)}, f32[7,32,8,128]{3,2,1,0:T(8,128)}, u32[]{:S(2)}) %copy-start) | copy-done | bytes 917528
  1.8 0.0 copy-start.2
  1.8 0.9 %copy-done.2 = f32[32,8,128]{2,1,0:T(8,128)S(1)} copy-done((f32[32,8,128]{2,1,0:T(8,128)S(1)}, f32[32,8,128]{2,1,0:T(8,128)}, u32[]{:S(2)}) %copy-start.2) | copy-done | bytes 131096
  2.7 0.0 copy-start.3
  2.7 0.9 %copy-done.3 = f32[32,8,128]{2,1,0:T(8,128)S(1)} copy-done((f32[32,8,128]{2,1,0:T(8,128)S(1)}, f32[32,8,128]{2,1,0:T(8,128)}, u32[]{:S(2)}) %copy-start.3) | copy-done | bytes 131096
  3.6 0.0 copy-start.4
  3.6 0.7 %copy-done.4 = f32[7,32]{1,0:T(8,128)S(1)} copy-done((f32[7,32]{1,0:T(8,128)S(1)}, f32[7,32]{1,0:T(8,128)}, u32[]{:S(2)}) %copy-start.4) | copy-done | bytes 920
  4.3 0.0 copy-start.1
  4.3 41.4 %exchange.1 = (f32[32,16,1,128]{3,2,1,0:T(1,128)S(1)}, f32[7,32,8,128]{3,2,1,0:T(8,128)S(1)}, f32[7,8,128]{2,1,0:T(8,128)S(1)}, f32[7,8,128]{2,1,0:T(8,128)S(1)}, f32[7,8,128]{2,1,0:T(8,128)S(1)}) custom-call(f32[32,8,128]{2,1,0:T(8,128)S(1)} %copy-done.2, f32[32,8,128]{2,1,0:T(8,128)S(1)} %copy-done.3, f32[7,32]{1,0:T(8,128)S(1)} %copy-done.4, ...), custom_call_target="tpu_custom_call" | custom-call | tf_op jit(solution)/shard_map/exchange/pallas_call | solution.py:175
  45.8 0.0 copy-done.1
  45.8 17.0 %solve.1 = (f32[7,32,8,128]{3,2,1,0:T(8,128)}, f32[8,128]{1,0:T(8,128)}) custom-call(f32[512,128]{1,0:T(8,128)S(1)} %bitcast.1, f32[7,8,128]{2,1,0:T(8,128)S(1)} %get-tuple-element.8.ent, f32[7,8,128]{2,1,0:T(8,128)S(1)} %get-tuple-element.9.ent_l, f32[7,8,128]{2,1,0:T(8,128)S(1)} %get-tuple-element.10.ent_r, f32[7,32]{1,0:T(8,128)S(1)} %copy-done.4, ...), custom_call_target="tpu_custom_call" | custom-call | tf_op jit(solution)/shard_map/solve/pallas_call | solution.py:568
Async XLA Ops:
  0.6 1.2 %copy-start = (f32[7,32,8,128]{3,2,1,0:T(8,128)S(1)}, f32[7,32,8,128]{3,2,1,0:T(8,128)}, u32[]{:S(2)}) copy-start(f32[7,32,8,128]{3,2,1,0:T(8,128)} %dens_hbm.1) | copy-start | bytes 2752516
  1.8 0.9 %copy-start.2 = (f32[32,8,128]{2,1,0:T(8,128)S(1)}, f32[32,8,128]{2,1,0:T(8,128)}, u32[]{:S(2)}) copy-start(f32[32,8,128]{2,1,0:T(8,128)} %ped.1) | copy-start | bytes 393220
  2.7 0.9 %copy-start.3 = (f32[32,8,128]{2,1,0:T(8,128)S(1)}, f32[32,8,128]{2,1,0:T(8,128)}, u32[]{:S(2)}) copy-start(f32[32,8,128]{2,1,0:T(8,128)} %wind.1) | copy-start | bytes 393220
  3.6 0.7 %copy-start.4 = (f32[7,32]{1,0:T(8,128)S(1)}, f32[7,32]{1,0:T(8,128)}, u32[]{:S(2)}) copy-start(f32[7,32]{1,0:T(8,128)} %cour.3) | copy-start | bytes 2692
  4.3 41.5 %copy-start.1 = (f32[7,32,8,128]{3,2,1,0:T(8,128)S(1)}, f32[7,32,8,128]{3,2,1,0:T(8,128)}, u32[]{:S(2)}) copy-start(f32[7,32,8,128]{3,2,1,0:T(8,128)} %dens_hbm.1) | copy-start | bytes 2752516
where the time goes:
time: 62.9 us; the launch traced here: 62.7 us
  Pallas kernels  58.4 us (93%)
  local copies, waits for them, and re-layouts  3.67 us (6%)
  between operations  0.66 us (1%)
    pallas_call x1, Pallas kernels, exchange(): pl.pallas_call(functools.partial(exchange_kernel, nt, nl), out_shape=(jax...  41.4 us
    pallas_call x1, Pallas kernels, solve(): pl.pallas_call(solve_kernel, out_shape=(jax.ShapeDtypeStruct(density.shap...  17 us
    unnamed x10, local copies, waits for them, and re-layouts  3.67 us

commit v1 on v0

--- a/solution.py
+++ b/solution.py
@@ -12,199 +12,8 @@
 CAP = 0.2
 NV = 32
 CYCLES = 3
+SCALE = 1.0 / 512.0
 MESH = pl.DeviceIdType.MESH
-
-
-def exchange_kernel(
-    nt, nl, ped, wind, cour, dens, gath, halo, ent, ent_l, ent_r,
-    part, recv1, row, recv2, dloc, atab, btab, bsend, brecv, psend,
-    s_ld, s_rs, r_rs, s_ag, r_ag, s_lg, r_lg, s_h, r_h, s_b, r_b, s_p, r_p, s_e, r_e,
-):
-    ns, pts = dens.shape[0], dens.shape[1]
-    rp = 16 // nt
-    t, l = lax.axis_index("tube"), lax.axis_index("lon")
-
-    load = pltpu.make_async_copy(dens, dloc, s_ld)
-    load.start()
-
-    barrier = pltpu.get_barrier_semaphore()
-    for o in range(1, nt):
-        pl.semaphore_signal(
-            barrier, inc=1, device_id=(lax.rem(t + o, nt), l), device_id_type=MESH
-        )
-    for o in range(1, nl):
-        pl.semaphore_signal(
-            barrier, inc=1, device_id=(t, lax.rem(l + o, nl)), device_id_type=MESH
-        )
-
-    csum = [ped[k] for k in range(4)]
-    ssum = [ped[k] * wind[k] for k in range(4)]
-    for p in range(4, pts):
-        csum[p % 4] = csum[p % 4] + ped[p]
-        ssum[p % 4] = ssum[p % 4] + ped[p] * wind[p]
-    csum = (csum[0] + csum[1]) + (csum[2] + csum[3])
-    ssum = (ssum[0] + ssum[1]) + (ssum[2] + ssum[3])
-    for r in range(8):
-        part[r // rp, r % rp, :] = csum[r]
-        part[(8 + r) // rp, r % rp, :] = ssum[r]
-
-    pl.semaphore_wait(barrier, nt + nl - 2)
-
-    def remote(src, dst, ssem, rsem, to):
-        c = pltpu.make_async_remote_copy(
-            src_ref=src, dst_ref=dst, send_sem=ssem, recv_sem=rsem,
-            device_id=to, device_id_type=MESH,
-        )
-        c.start()
-        return c
-
-    rs = []
-    for o in range(1, nt):
-        to = lax.rem(t + o, nt)
-        rs.append(remote(part.at[to], recv1.at[o], s_rs.at[o], r_rs.at[o], (to, l)))
-    recv1[0] = part[t]
-
-    right, left = lax.rem(l + 1, nl), lax.rem(l + nl - 1, nl)
-    h0 = remote(
-        dens.at[:, :, pl.ds(7, 1), :], halo.at[:, :, pl.ds(0, 1), :], s_h.at[0], r_h.at[0], (t, right)
-    )
-    h1 = remote(
-        dens.at[:, :, pl.ds(0, 1), :], halo.at[:, :, pl.ds(7, 1), :], s_h.at[1], r_h.at[1], (t, left)
-    )
-
-    coefficient_tables(cour, atab, btab)
-    load.wait()
-
-    def step(p, carry):
-        out = []
-        for s in range(ns):
-            x, m = carry[s]
-            a, b = row_of(atab, p * 8 + s), row_of(btab, p * 8 + s)
-            out.append((a * x + b * dloc[s, p], a * m))
-        return tuple(out)
-
-    zero, one = jnp.zeros((8, 128), F32), jnp.ones((8, 128), F32)
-    ends = lax.fori_loop(0, pts, step, tuple((zero, one) for _ in range(ns)))
-    for s in range(ns):
-        bsend[s, 0] = ends[s][0]
-        bsend[s, 1] = ends[s][1]
-
-    for c in rs:
-        c.wait_recv()
-    total = recv1[0]
-    for o in range(1, nt):
-        total = total + recv1[o]
-    row[...] = total
-    ag = []
-    for o in range(1, nt):
-        to = lax.rem(t + o, nt)
-        ag.append(remote(row, recv2.at[t], s_ag.at[o], r_ag.at[o], (to, l)))
-    recv2[t] = total
-
-    mine = (t * ns + nt - 1) // nt
-    owner_of = [(s * nt) // ns for s in range(ns)]
-    is_owner = jnp.logical_and(mine < ns, (mine * nt) // ns == t)
-    for s in range(ns):
-
-        @pl.when(t != owner_of[s])
-        def _():
-            o = lax.rem(t - owner_of[s] + nt, nt)
-            remote(bsend.at[s], brecv.at[o], s_b.at[s], r_b.at[o], (owner_of[s], l))
-
-    for c in ag:
-        c.wait_recv()
-    own = pltpu.make_async_copy(recv2, gath.at[l], s_lg.at[0])
-    own.start()
-    lg = []
-    for o in range(1, nl):
-        to = lax.rem(l + o, nl)
-        lg.append(remote(recv2, gath.at[l], s_lg.at[o], r_lg.at[o], (t, to)))
-
-    @pl.when(is_owner)
-    def _():
-        brecv[0] = bsend[mine]
-        for o in range(1, nt):
-            pltpu.make_async_copy(brecv.at[o], brecv.at[o], r_b.at[o]).wait()
-        x = zero
-        for k in range(nt):
-            psend[k] = x
-            o = lax.rem(k - t + nt, nt)
-            x = brecv[o, 1] * x + brecv[o, 0]
-        ent[mine] = psend[t]
-        for o in range(1, nt):
-            to = lax.rem(t + o, nt)
-            remote(psend.at[to], ent.at[mine], s_p.at[o], r_p.at[mine], (to, l))
-
-    for s in range(ns):
-
-        @pl.when(t != owner_of[s])
-        def _():
-            pltpu.make_async_copy(ent.at[s], ent.at[s], r_p.at[s]).wait()
-
-    e0 = remote(ent, ent_l, s_e.at[0], r_e.at[0], (t, right))
-    e1 = remote(ent, ent_r, s_e.at[1], r_e.at[1], (t, left))
-
-    own.wait()
-    for c in rs + ag + lg:
-        c.wait_send()
-    for c in lg:
-        c.wait_recv()
-    for s in range(ns):
-
-        @pl.when(t != owner_of[s])
-        def _():
-            pltpu.make_async_copy(bsend.at[s], bsend.at[s], s_b.at[s]).wait()
-
-    @pl.when(is_owner)
-    def _():
-        for o in range(1, nt):
-            pltpu.make_async_copy(psend.at[0], psend.at[0], s_p.at[o]).wait()
-
-    for c in (h0, h1, e0, e1):
-        c.wait()
-
-
-def exchange(mesh, density, pedersen, wind, courant):
-    nt, nl = mesh.shape["tube"], mesh.shape["lon"]
-    ns, pts = density.shape[:2]
-    rp = 16 // nt
-    vm = pl.BlockSpec(memory_space=pltpu.VMEM)
-    hbm = pl.BlockSpec(memory_space=pl.ANY)
-    dma = pltpu.SemaphoreType.DMA
-    state = jax.ShapeDtypeStruct((ns, 8, 128), F32)
-    return pl.pallas_call(
-        functools.partial(exchange_kernel, nt, nl),
-        out_shape=(
-            jax.ShapeDtypeStruct((nl, nt, rp, 128), F32),
-            jax.ShapeDtypeStruct(density.shape, F32),
-            state, state, state,
-        ),
-        in_specs=[vm, vm, vm, hbm],
-        out_specs=(vm, hbm, vm, vm, vm),
-        scratch_shapes=[
-            pltpu.VMEM((nt, rp, 128), F32),
-            pltpu.VMEM((nt, rp, 128), F32),
-            pltpu.VMEM((rp, 128), F32),
-            pltpu.VMEM((nt, rp, 128), F32),
-            pltpu.VMEM(density.shape, F32),
-            pltpu.VMEM((pts * 8, 128), F32),
-            pltpu.VMEM((pts * 8, 128), F32),
-            pltpu.VMEM((ns, 2, 8, 128), F32),
-            pltpu.VMEM((nt, 2, 8, 128), F32),
-            pltpu.VMEM((nt, 8, 128), F32),
-            dma,
-            dma((nt,)), dma((nt,)), dma((nt,)), dma((nt,)),
-            dma((nl,)), dma((nl,)),
-            dma((2,)), dma((2,)),
-            dma((ns,)), dma((nt,)),
-            dma((nt,)), dma((ns,)),
-            dma((2,)), dma((2,)),
-        ],
-        compiler_params=pltpu.CompilerParams(
-            collective_id=0, has_side_effects=True, vmem_limit_bytes=40 * 2**20
-        ),
-        name="exchange",
-    )(pedersen, wind, courant, density)
 
 
 def row_of(ref, r):
@@ -462,29 +271,39 @@
     return x
 
 
-def potential_of(gath, w, sq, sq2, bmat, emat, gs, xs, xts, left, pivots, vecs):
-    scale = 1.0 / 512.0
-    at = [pl.ds((v // 8) * 16 + v % 8, 8, stride=64) for v in range(NV)]
-    cond = [gath[s, :] * scale for s in at]
+def conductance_setup(gath, w, ring, mats):
+    cond = [gath[pl.ds((v // 8) * 16 + v % 8, 8, stride=64), :] * SCALE for v in range(NV)]
     level_weights(cond, 0, *w[0])
     c = coarsened(cond, 1)
     level_weights(c, 1, *w[1])
     c = coarsened(c, 2)
     level_weights(c, 2, *w[2])
     c = coarsened(c, 4)
+    sq, sq2, vecs = ring
+    bmat, emat, gs, xs, xts, left, pivots = mats
     ring_matrix(to_ring(c, sq, sq2), bmat, emat)
     factor(bmat, emat, gs, xs, xts, left, pivots)
-    at = [pl.ds((v // 8) * 16 + 8 + v % 8, 8, stride=64) for v in range(NV)]
-    source = [gath[s, :] * scale for s in at]
+
+
+def cycles(gath, w, ring, mats, pot):
+    sq, sq2, vecs = ring
+    _, _, gs, xs, xts, _, _ = mats
 
     def coarse(r):
         x = ring_solve(to_ring(r, sq, sq2), gs, xs, xts, vecs)
         return from_ring(x, sq, sq2, vecs.at[16])
 
-    x = None
-    for _ in range(CYCLES):
-        x = vcycle(0, source, x, w, coarse)
-    return x
+    def body(_, carry):
+        at = [pl.ds((v // 8) * 16 + 8 + v % 8, 8, stride=64) for v in range(NV)]
+        source = [gath[s, :] * SCALE for s in at]
+        x = vcycle(0, source, [pot[v] for v in range(NV)], w, coarse)
+        for v in range(NV):
+            pot[v] = x[v]
+        return carry
+
+    for v in range(NV):
+        pot[v] = jnp.zeros((8, 128), F32)
+    lax.fori_loop(0, CYCLES, body, 0)
 
 
 def stencil(pot, west, east):
@@ -505,33 +324,224 @@
     return centre, pos[0], -neg[1], pos[2], -neg[3]
 
 
-def solve_kernel(
-    gath, ent, ent_l, ent_r, cour, dens_hbm, halo_hbm, out, pot,
+def dynamo_kernel(
+    nt, nl, ped_hbm, wind_hbm, cour_hbm, dens_hbm,
+    coef, pot_own, ent, ent_l, ent_r, dens, halo, atab, btab,
+    ped, wind, cour, part, parts, gath, bsend, brecv, psend,
     wl0, ws0, wn0, kk0, dd0, wl1, ws1, wn1, kk1, wl2, ws2, wn2, kk2,
-    sq, sq2, bmat, emat, gs, xs, xts, left, pivots, vecs, whole, atab, btab, dens, halo, sem,
+    sq, sq2, bmat, emat, gs, xs, xts, left, pivots, vecs, pot, whole,
+    s_ld, s_t, r_t, s_l, r_l, s_h, r_h, s_b, r_b, s_p, r_p, s_e, r_e,
 ):
-    ns, pts = out.shape[:2]
-    l = lax.axis_index("lon")
+    ns, pts = dens.shape[:2]
+    t, l = lax.axis_index("tube"), lax.axis_index("lon")
     loads = [
-        pltpu.make_async_copy(dens_hbm, dens, sem.at[0]),
-        pltpu.make_async_copy(halo_hbm, halo, sem.at[1]),
+        pltpu.make_async_copy(src, dst, s_ld.at[k])
+        for k, (src, dst) in enumerate(
+            ((ped_hbm, ped), (wind_hbm, wind), (cour_hbm, cour), (dens_hbm, dens))
+        )
     ]
     for c in loads:
         c.start()
+
+    far_t = sorted(range(1, nt), key=lambda o: -min(o, nt - o))
+    far_l = sorted(range(1, nl), key=lambda o: -min(o // 2 % 4, 4 - o // 2 % 4) - min(o // 8, 4 - o // 8))
+    barrier = pltpu.get_barrier_semaphore()
+    for o in far_t:
+        pl.semaphore_signal(
+            barrier, inc=1, device_id=(lax.rem(t + o, nt), l), device_id_type=MESH
+        )
+    for o in far_l:
+        pl.semaphore_signal(
+            barrier, inc=1, device_id=(t, lax.rem(l + o, nl)), device_id_type=MESH
+        )
+
+    loads[0].wait()
+    loads[1].wait()
+    csum = [ped[k] for k in range(4)]
+    ssum = [ped[k] * wind[k] for k in range(4)]
+    for p in range(4, pts):
+        csum[p % 4] = csum[p % 4] + ped[p]
+        ssum[p % 4] = ssum[p % 4] + ped[p] * wind[p]
+    part[pl.ds(0, 8), :] = (csum[0] + csum[1]) + (csum[2] + csum[3])
+    part[pl.ds(8, 8), :] = (ssum[0] + ssum[1]) + (ssum[2] + ssum[3])
+
+    def remote(src, dst, ssem, rsem, to):
+        c = pltpu.make_async_remote_copy(
+            src_ref=src, dst_ref=dst, send_sem=ssem, recv_sem=rsem,
+            device_id=to, device_id_type=MESH,
+        )
+        c.start()
+        return c
+
+    pl.semaphore_wait(barrier, nt + nl - 2)
+    along = []
+    for o in far_t:
+        to = lax.rem(t + o, nt)
+        along.append(remote(part, parts.at[o], s_t.at[o], r_t.at[o], (to, l)))
+
+    right, left_l = lax.rem(l + 1, nl), lax.rem(l + nl - 1, nl)
+    h0 = remote(
+        dens_hbm.at[:, :, pl.ds(7, 1), :], halo.at[:, :, pl.ds(0, 1), :], s_h.at[0], r_h.at[0], (t, right)
+    )
+    h1 = remote(
+        dens_hbm.at[:, :, pl.ds(0, 1), :], halo.at[:, :, pl.ds(7, 1), :], s_h.at[1], r_h.at[1], (t, left_l)
+    )
+
+    loads[2].wait()
     coefficient_tables(cour, atab, btab)
+    loads[3].wait()
+
+    def step(p, carry):
+        out = []
+        for s in range(ns):
+            x, m = carry[s]
+            a, b = row_of(atab, p * 8 + s), row_of(btab, p * 8 + s)
+            out.append((a * x + b * dens[s, p], a * m))
+        return tuple(out)
+
+    zero, one = jnp.zeros((8, 128), F32), jnp.ones((8, 128), F32)
+    ends = lax.fori_loop(0, pts, step, tuple((zero, one) for _ in range(ns)))
+    for s in range(ns):
+        bsend[s, 0] = ends[s][0]
+        bsend[s, 1] = ends[s][1]
+
+    mine = (t * ns + nt - 1) // nt
+    owner_of = [(s * nt) // ns for s in range(ns)]
+    is_owner = jnp.logical_and(mine < ns, (mine * nt) // ns == t)
+    for s in range(ns):
+
+        @pl.when(t != owner_of[s])
+        def _():
+            o = lax.rem(t - owner_of[s] + nt, nt)
+            remote(bsend.at[s], brecv.at[o], s_b.at[s], r_b.at[o], (owner_of[s], l))
+
+    parts[0] = part[...]
+    total = None
+    for c in reversed(along):
+        c.wait_recv()
+    for o in range(nt):
+        total = parts[o] if total is None else total + parts[o]
+    gath[pl.ds(pl.multiple_of(l * 16, 16), 16), :] = total
+    mine_rows = gath.at[pl.ds(pl.multiple_of(l * 16, 16), 16), :]
+    across = []
+    for o in far_l:
+        to = lax.rem(l + o, nl)
+        across.append(remote(mine_rows, mine_rows, s_l.at[o], r_l.at[o], (t, to)))
+
+    @pl.when(is_owner)
+    def _():
+        brecv[0] = bsend[mine]
+        for o in range(1, nt):
+            pltpu.make_async_copy(brecv.at[o], brecv.at[o], r_b.at[o]).wait()
+        x = zero
+        for k in range(nt):
+            psend[k] = x
+            o = lax.rem(k - t + nt, nt)
+            x = brecv[o, 1] * x + brecv[o, 0]
+        ent[mine] = psend[t]
+        for o in far_t:
+            to = lax.rem(t + o, nt)
+            remote(psend.at[to], ent.at[mine], s_p.at[o], r_p.at[mine], (to, l))
+
+    for c in across:
+        c.wait_recv()
+
     w = [(wl0, ws0, wn0, kk0, dd0), (wl1, ws1, wn1, kk1, None), (wl2, ws2, wn2, kk2, None)]
-    x = potential_of(gath, w, sq, sq2, bmat, emat, gs, xs, xts, left, pivots, vecs)
+    ring, mats = (sq, sq2, vecs), (bmat, emat, gs, xs, xts, left, pivots)
+    conductance_setup(gath, w, ring, mats)
+
+    for s in range(ns):
+
+        @pl.when(t != owner_of[s])
+        def _():
+            pltpu.make_async_copy(ent.at[s], ent.at[s], r_p.at[s]).wait()
+
+    e0 = remote(ent, ent_l, s_e.at[0], r_e.at[0], (t, right))
+    e1 = remote(ent, ent_r, s_e.at[1], r_e.at[1], (t, left_l))
+
+    cycles(gath, w, ring, mats, pot)
     for v in range(NV):
-        whole[pl.ds(v, 8, stride=NV), :] = x[v]
+        whole[pl.ds(v, 8, stride=NV), :] = pot[v]
     own = whole[pl.ds(pl.multiple_of(l * 8, 8), 8), :]
     sub = lax.broadcasted_iota(jnp.int32, (8, 128), 0)
     west = jnp.where(sub == 0, row_of(whole, lax.rem(l * 8 + 255, 256)), pltpu.roll(own, 1, 0))
     east = jnp.where(sub == 7, row_of(whole, lax.rem(l * 8 + 8, 256)), pltpu.roll(own, 7, 0))
-    pot[...] = own
-    cc, cw, ce, cs, cn = stencil(own, west, east)
-    for c in loads:
+    pot_own[...] = own
+    for k, c in enumerate(stencil(own, west, east)):
+        coef[k] = c
+
+    for c in along + across:
+        c.wait_send()
+    for s in range(ns):
+
+        @pl.when(t != owner_of[s])
+        def _():
+            pltpu.make_async_copy(bsend.at[s], bsend.at[s], s_b.at[s]).wait()
+
+    @pl.when(is_owner)
+    def _():
+        for o in range(1, nt):
+            pltpu.make_async_copy(psend.at[0], psend.at[0], s_p.at[o]).wait()
+
+    for c in (h0, h1, e0, e1):
         c.wait()
 
+
+VM = pl.BlockSpec(memory_space=pltpu.VMEM)
+HBM = pl.BlockSpec(memory_space=pltpu.HBM)
+
+
+def tiles(*n):
+    return pltpu.VMEM((*n, 8, 128), F32)
+
+
+def rows(n):
+    return pltpu.VMEM((n, 128), F32)
+
+
+def dynamo(mesh, density, pedersen, wind, courant):
+    nt, nl = mesh.shape["tube"], mesh.shape["lon"]
+    ns, pts = density.shape[:2]
+    dma = pltpu.SemaphoreType.DMA
+    state = jax.ShapeDtypeStruct((ns, 8, 128), F32)
+    table = jax.ShapeDtypeStruct((pts * 8, 128), F32)
+    levels = [tiles(33)] + [tiles(32)] * 4 + [tiles(17)] + [tiles(16)] * 3 + [tiles(9)] + [tiles(8)] * 3
+    return pl.pallas_call(
+        functools.partial(dynamo_kernel, nt, nl),
+        out_shape=(
+            jax.ShapeDtypeStruct((5, 8, 128), F32),
+            jax.ShapeDtypeStruct((8, 128), F32),
+            state, state, state,
+            jax.ShapeDtypeStruct(density.shape, F32),
+            jax.ShapeDtypeStruct(density.shape, F32),
+            table, table,
+        ),
+        in_specs=[HBM] * 4,
+        out_specs=(VM,) * 9,
+        scratch_shapes=[
+            tiles(pts), tiles(pts), pltpu.VMEM((ns, pts), F32),
+            rows(16), pltpu.VMEM((nt, 16, 128), F32), rows(512),
+            tiles(ns, 2), tiles(nt, 2), tiles(nt),
+        ]
+        + levels
+        + [rows(128), rows(128), rows(256), rows(256), rows(6 * 256), rows(5 * 256), rows(5 * 256)]
+        + [rows(256), rows(256), pltpu.VMEM((17, 16, 128), F32), tiles(NV), rows(256)]
+        + [
+            dma((4,)), dma((nt,)), dma((nt,)), dma((nl,)), dma((nl,)), dma((2,)), dma((2,)),
+            dma((ns,)), dma((nt,)), dma((nt,)), dma((ns,)), dma((2,)), dma((2,)),
+        ],
+        compiler_params=pltpu.CompilerParams(
+            collective_id=0, has_side_effects=True, vmem_limit_bytes=40 * 2**20
+        ),
+        name="dynamo",
+    )(pedersen, wind, courant, density)
+
+
+def transport_kernel(coef, pot_in, ent, ent_l, ent_r, dens, halo, atab, btab, out, pot):
+    ns, pts = out.shape[:2]
+    pot[...] = pot_in[...]
+    cc, cw, ce, cs, cn = (coef[k] for k in range(5))
+    sub = lax.broadcasted_iota(jnp.int32, (8, 128), 0)
     start = []
     for s in range(ns):
         side = jnp.where(sub == 0, pltpu.roll(ent_l[s], 1, 0), pltpu.roll(ent_r[s], 7, 0))
@@ -553,41 +563,25 @@
     lax.fori_loop(0, pts, step, tuple(start))
 
 
-def solve(gath, ent, ent_l, ent_r, courant, density, halo):
-    ns, pts = density.shape[:2]
-    vm = pl.BlockSpec(memory_space=pltpu.VMEM)
-    hbm = pl.BlockSpec(memory_space=pl.ANY)
-
-    def tiles(n):
-        return pltpu.VMEM((n, 8, 128), F32)
-
-    def rows(n):
-        return pltpu.VMEM((n, 128), F32)
-
-    levels = [tiles(33)] + [tiles(32)] * 4 + [tiles(17)] + [tiles(16)] * 3 + [tiles(9)] + [tiles(8)] * 3
+def transport(coef, pot, ent, ent_l, ent_r, density, halo, atab, btab):
     return pl.pallas_call(
-        solve_kernel,
+        transport_kernel,
         out_shape=(
             jax.ShapeDtypeStruct(density.shape, F32),
             jax.ShapeDtypeStruct((8, 128), F32),
         ),
-        in_specs=[vm] * 5 + [hbm] * 2,
-        out_specs=(vm, vm),
-        scratch_shapes=levels
-        + [rows(128), rows(128), rows(256), rows(256), rows(6 * 256), rows(5 * 256), rows(5 * 256)]
-        + [rows(256), rows(256), pltpu.VMEM((17, 16, 128), F32), rows(256)]
-        + [rows(pts * 8), rows(pts * 8)]
-        + [pltpu.VMEM(density.shape, F32), pltpu.VMEM(density.shape, F32)]
-        + [pltpu.SemaphoreType.DMA((2,))],
-        compiler_params=pltpu.CompilerParams(vmem_limit_bytes=40 * 2**20),
-        name="solve",
-    )(gath, ent, ent_l, ent_r, courant, density, halo)
+        in_specs=[VM] * 9,
+        out_specs=(VM, VM),
+        compiler_params=pltpu.CompilerParams(vmem_limit_bytes=24 * 2**20),
+        name="transport",
+    )(coef, pot, ent, ent_l, ent_r, density, halo, atab, btab)
 
 
 def solution(mesh):
     def on_device(density, pedersen, wind, courant):
-        gath, halo, ent, ent_l, ent_r = exchange(mesh, density, pedersen, wind, courant)
-        return solve(gath.reshape(-1, 128), ent, ent_l, ent_r, courant, density, halo)
+        args = (density, pedersen, wind, courant)
+        args = (pltpu.with_memory_space_constraint(x, pltpu.HBM) for x in args)
+        return transport(*dynamo(mesh, *args))
 
     return jax.shard_map(
         on_device,

time: 62.9 us -> 52.5 us (0.83)
  Pallas kernels: 58.4 us -> 51.7 us
  local copies, waits for them, and re-layouts: 3.67 us -> 0 us
    pallas_call x2, Pallas kernels: 58.4 us -> 51.7 us  [the longest x1 47.9 us: dynamo(): pl.pallas_call(functools.partial(dynamo_kernel, nt, nl), out_shape=(jax.S...]
    unnamed x10 -> x0, local copies, waits for them, and re-layouts: 3.67 us -> none
where the time goes in v1:
time: 52.5 us; the launch traced here: 52.3 us
  Pallas kernels  51.7 us (98%)
  between operations  0.64 us (1%)
    pallas_call x1, Pallas kernels, dynamo(): pl.pallas_call(functools.partial(dynamo_kernel, nt, nl), out_shape=(jax.S...  47.9 us
    pallas_call x1, Pallas kernels, transport(): pl.pallas_call(transport_kernel, out_shape=(jax.ShapeDtypeStruct(density....  3.77 us

profile of v1, /device:TPU:1, one launch (start us, length us, event | category | flops | bytes accessed | tf_op | source)
XLA Modules:
  0.0 52.3 jit_solution(13255765193553101558)
XLA Ops:
  0.6 47.9 %dynamo.1 = (f32[5,8,128]{2,1,0:T(8,128)S(1)}, f32[8,128]{1,0:T(8,128)S(1)}, f32[7,8,128]{2,1,0:T(8,128)S(1)}, f32[7,8,128]{2,1,0:T(8,128)S(1)}, f32[7,8,128]{2,...) custom-call(f32[32,8,128]{2,1,0:T(8,128)} %ped_hbm.1, ...), custom_call_target="tpu_custom_call" | custom-call | tf_op jit(solution)/shard_map/dynamo/pallas_call | solution.py:509
  48.6 3.8 %transport.1 = (f32[7,32,8,128]{3,2,1,0:T(8,128)}, f32[8,128]{1,0:T(8,128)}) custom-call(f32[5,8,128]{2,1,0:T(8,128)S(1)} %get-tuple-element.11.coef, f32[8,128]{1,0:T(8,128)S(1)} %get-tuple-element.12.pot_in, f32[7,8,128]{2,1,0:T(8,128)S(1)} %get-tuple-element.13.ent, f32[7,8,128]{2,1,0:T(8,128)S(1)} %get-tuple-element.14.ent_l, ...), custom_call_target="tpu_custom_call" | custom-call | tf_op jit(solution)/shard_map/transport/pallas_call | solution.py:567

commit v2 on v1

--- a/solution.py
+++ b/solution.py
@@ -180,64 +180,72 @@
             ref[pl.ds(base + i * 16 + h * 8, 8), :] = a[i][h]
 
 
-def product(left, rights):
-    outs = [[] for _ in rights]
+def packed_product(left, right, count):
+    out = []
     for i in range(16):
-        acc = [[None, None] for _ in rights]
-        for k in range(16):
-            f = row_of(left, i * 16 + k)
-            for q, right in enumerate(rights):
-                for h in range(2):
-                    term = f * right[k][h]
-                    acc[q][h] = term if k == 0 else acc[q][h] + term
-        for q in range(len(rights)):
-            outs[q].append(acc[q])
-    return outs
-
-
-def factor(bmat, emat, gs, xs, xts, left, pivots):
+        acc = [row_of(left, i * 16 + k) * right[k] for k in range(count)]
+        while len(acc) > 1:
+            acc = [acc[q] + acc[q + 1] for q in range(0, len(acc), 2)]
+        out.append(acc[0])
+    return out
+
+
+def factor(bmat, emat, ps, qs, gf, left, left2, pivots):
     lane = lax.broadcasted_iota(jnp.int32, (8, 128), 1)
+    group = lane // 32
     both = [(i, h) for i in range(16) for h in range(2)]
+    two = range(2)
+
+    def by_group(a, b, c, d):
+        return jnp.where(group < 2, jnp.where(group == 0, a, b), jnp.where(group == 2, c, d))
+
+    def spread(y):
+        r = [y] + [lroll(y, 32 * q) for q in range(1, 4)]
+        return [by_group(*(r[(g - c) % 4] for g in range(4))) for c in range(4)]
 
     def body(m, _):
         d = jnp.left_shift(1, m)
-        odd = jnp.bitwise_and(lane, d) != 0
         base = pl.multiple_of(m * 256, 256)
-        g = inverted([[mat(bmat, i, h) for h in range(2)] for i in range(16)], pivots)
-        put(gs, g, base)
 
         def ahead(x):
             return pltpu.roll(x, 128 - d, 1)
 
+        def behind(x):
+            return pltpu.roll(x, d, 1)
+
+        g = inverted([[mat(bmat, i, h) for h in two] for i in range(16)], pivots)
+        u = [[mat(emat, i, h) for h in two] for i in range(16)]
+        ut = [[matT(emat, i, h) for h in two] for i in range(16)]
         for i, h in both:
-            left[pl.ds(i * 16 + h * 8, 8), :] = jnp.where(odd, g[i][h], ahead(g[i][h]))
-        f = [
-            [jnp.where(odd, mat(emat, i, h), matT(emat, i, h)) for h in range(2)] for i in range(16)
+            left[pl.ds(i * 16 + h * 8, 8), :] = jnp.where(group < 2, g[i][h], ahead(g[i][h]))
+        for i in range(16):
+            left2[pl.ds(i * 16, 8), :] = jnp.where(group < 2, ut[i][0], ut[i][1])
+        quarters = [
+            spread(y)
+            for y in packed_product(left, [by_group(*u[k], *ut[k]) for k in range(16)], 16)
         ]
-        (x,) = product(left, [f])
-        put(xs, x, base)
+        q = [y[:2] for y in quarters]
+        p = [y[2:] for y in quarters]
+        put(ps, p, base)
+        put(qs, [[behind(q[i][h]) for h in two] for i in range(16)], base)
+        right = [by_group(*p[k], *(ahead(q[k][h]) for h in two)) for k in range(16)]
+        first = [spread(y) for y in packed_product(emat, right, 16)]
+        right = [by_group(*q[k], *q[k + 8]) for k in range(8)]
+        second = []
+        for y in packed_product(left2, right, 8):
+            y = y + lroll(y, 64)
+            z = lroll(y, 32)
+            flip = group % 2 == 0
+            second.append([jnp.where(flip, y, z), jnp.where(flip, z, y)])
         for i, h in both:
-            xts[pl.ds(base + i * 16 + h * 8, 8), :] = xs[pl.ds(base + h * 128 + i, 8, stride=16), :]
-        for i, h in both:
-            left[pl.ds(i * 16 + h * 8, 8), :] = jnp.where(odd, matT(emat, i, h), mat(emat, i, h))
-        y, n = product(left, [x, [[ahead(x[i][h]) for h in range(2)] for i in range(16)]])
-        even = jnp.bitwise_and(lane, 2 * d - 1) == 0
-        for i, h in both:
-            old = mat(bmat, i, h)
-            fresh = old - (y[i][h] + pltpu.roll(y[i][h], d, 1))
-            bmat[pl.ds(i * 16 + h * 8, 8), :] = jnp.where(even, fresh, old)
-            emat[pl.ds(i * 16 + h * 8, 8), :] = -n[i][h]
+            rows_at = pl.ds(i * 16 + h * 8, 8)
+            bmat[rows_at, :] = bmat[rows_at, :] - (first[i][h] + behind(second[i][h]))
+            emat[rows_at, :] = -first[i][2 + h]
         return 0
 
     lax.fori_loop(0, 5, body, 0)
-    last = [
-        [mat(bmat, i, h) + (mat(emat, i, h) + matT(emat, i, h)) for h in range(2)] for i in range(16)
-    ]
-    even = jnp.bitwise_and(lane, 31) == 0
-    last = [
-        [jnp.where(even, last[i][h], mat(bmat, i, h)) for h in range(2)] for i in range(16)
-    ]
-    put(gs, inverted(last, pivots), 5 * 256)
+    last = [[mat(bmat, i, h) + (mat(emat, i, h) + matT(emat, i, h)) for h in two] for i in range(16)]
+    put(gf, inverted(last, pivots))
 
 
 def times(ref, base, vec, x):
@@ -251,24 +259,13 @@
     return out
 
 
-def ring_solve(r, gs, xs, xts, vecs):
-    lane = lax.broadcasted_iota(jnp.int32, (8, 128), 1)
-    two = range(2)
+def ring_solve(r, ps, qs, gf, vecs):
     for m in range(5):
         d = 1 << m
-        odd, even = (lane & d) != 0, (lane & (2 * d - 1)) == 0
-        sel = [jnp.where(odd, r[h], lroll(r[h], -d)) for h in two]
-        z = times(xs, m * 256, vecs.at[m], sel)
-        r = [jnp.where(even, r[h] - (z[h] + lroll(z[h], d)), r[h]) for h in two]
-    x = times(gs, 5 * 256, vecs.at[5], r)
-    for m in reversed(range(5)):
-        d = 1 << m
-        odd, now = (lane & d) != 0, (lane & (2 * d - 1)) == d
-        sel = [jnp.where(odd, lroll(x[h], -d), x[h]) for h in two]
-        g = times(gs, m * 256, vecs.at[6 + m], r)
-        q = times(xts, m * 256, vecs.at[11 + m], sel)
-        x = [jnp.where(now, g[h] - (q[h] + lroll(q[h], d)), x[h]) for h in two]
-    return x
+        p = times(ps, m * 256, vecs.at[2 * m], [lroll(r[h], -d) for h in range(2)])
+        q = times(qs, m * 256, vecs.at[2 * m + 1], [lroll(r[h], d) for h in range(2)])
+        r = [r[h] - (p[h] + q[h]) for h in range(2)]
+    return times(gf, 0, vecs.at[10], r)
 
 
 def conductance_setup(gath, w, ring, mats):
@@ -280,18 +277,18 @@
     level_weights(c, 2, *w[2])
     c = coarsened(c, 4)
     sq, sq2, vecs = ring
-    bmat, emat, gs, xs, xts, left, pivots = mats
+    bmat, emat, ps, qs, gf, left, left2, pivots = mats
     ring_matrix(to_ring(c, sq, sq2), bmat, emat)
-    factor(bmat, emat, gs, xs, xts, left, pivots)
+    factor(bmat, emat, ps, qs, gf, left, left2, pivots)
 
 
 def cycles(gath, w, ring, mats, pot):
     sq, sq2, vecs = ring
-    _, _, gs, xs, xts, _, _ = mats
+    ps, qs, gf = mats[2:5]
 
     def coarse(r):
-        x = ring_solve(to_ring(r, sq, sq2), gs, xs, xts, vecs)
-        return from_ring(x, sq, sq2, vecs.at[16])
+        x = ring_solve(to_ring(r, sq, sq2), ps, qs, gf, vecs)
+        return from_ring(x, sq, sq2, vecs.at[11])
 
     def body(_, carry):
         at = [pl.ds((v // 8) * 16 + 8 + v % 8, 8, stride=64) for v in range(NV)]
@@ -329,7 +326,7 @@
     coef, pot_own, ent, ent_l, ent_r, dens, halo, atab, btab,
     ped, wind, cour, part, parts, gath, bsend, brecv, psend,
     wl0, ws0, wn0, kk0, dd0, wl1, ws1, wn1, kk1, wl2, ws2, wn2, kk2,
-    sq, sq2, bmat, emat, gs, xs, xts, left, pivots, vecs, pot, whole,
+    sq, sq2, bmat, emat, ps, qs, gf, left, left2, pivots, vecs, pot, whole,
     s_ld, s_t, r_t, s_l, r_l, s_h, r_h, s_b, r_b, s_p, r_p, s_e, r_e,
 ):
     ns, pts = dens.shape[:2]
@@ -447,7 +444,7 @@
         c.wait_recv()
 
     w = [(wl0, ws0, wn0, kk0, dd0), (wl1, ws1, wn1, kk1, None), (wl2, ws2, wn2, kk2, None)]
-    ring, mats = (sq, sq2, vecs), (bmat, emat, gs, xs, xts, left, pivots)
+    ring, mats = (sq, sq2, vecs), (bmat, emat, ps, qs, gf, left, left2, pivots)
     conductance_setup(gath, w, ring, mats)
 
     for s in range(ns):
@@ -524,8 +521,8 @@
             tiles(ns, 2), tiles(nt, 2), tiles(nt),
         ]
         + levels
-        + [rows(128), rows(128), rows(256), rows(256), rows(6 * 256), rows(5 * 256), rows(5 * 256)]
-        + [rows(256), rows(256), pltpu.VMEM((17, 16, 128), F32), tiles(NV), rows(256)]
+        + [rows(128), rows(128), rows(256), rows(256), rows(5 * 256), rows(5 * 256), rows(256)]
+        + [rows(256), rows(256), rows(256), pltpu.VMEM((12, 16, 128), F32), tiles(NV), rows(256)]
         + [
             dma((4,)), dma((nt,)), dma((nt,)), dma((nl,)), dma((nl,)), dma((2,)), dma((2,)),
             dma((ns,)), dma((nt,)), dma((nt,)), dma((ns,)), dma((2,)), dma((2,)),

time: 52.5 us -> 49.2 us (0.937)
  Pallas kernels: 51.7 us -> 48.4 us
    pallas_call x1, Pallas kernels: 47.9 us -> 44.6 us  [dynamo(): pl.pallas_call(functools.partial(dynamo_kernel, nt, nl), out_shape=(jax.S...]
where the time goes in v2:
time: 49.2 us; the launch traced here: 49 us
  Pallas kernels  48.4 us (98%)
  between operations  0.64 us (1%)
    pallas_call x1, Pallas kernels, dynamo(): pl.pallas_call(functools.partial(dynamo_kernel, nt, nl), out_shape=(jax.S...  44.6 us
    pallas_call x1, Pallas kernels, transport(): pl.pallas_call(transport_kernel, out_shape=(jax.ShapeDtypeStruct(density....  3.77 us

profile of v2, /device:TPU:1, one launch (start us, length us, event | category | flops | bytes accessed | tf_op | source)
XLA Modules:
  0.0 49.0 jit_solution(17121740007994761301)
XLA Ops:
  0.6 44.6 %dynamo.1 = (f32[5,8,128]{2,1,0:T(8,128)S(1)}, f32[8,128]{1,0:T(8,128)S(1)}, f32[7,8,128]{2,1,0:T(8,128)S(1)}, f32[7,8,128]{2,1,0:T(8,128)S(1)}, f32[7,8,128]{2,...) custom-call(f32[32,8,128]{2,1,0:T(8,128)} %ped_hbm.1, ...), custom_call_target="tpu_custom_call" | custom-call | tf_op jit(solution)/shard_map/dynamo/pallas_call | solution.py:506
  45.3 3.8 %transport.1 = (f32[7,32,8,128]{3,2,1,0:T(8,128)}, f32[8,128]{1,0:T(8,128)}) custom-call(f32[5,8,128]{2,1,0:T(8,128)S(1)} %get-tuple-element.11.coef, f32[8,128]{1,0:T(8,128)S(1)} %get-tuple-element.12.pot_in, f32[7,8,128]{2,1,0:T(8,128)S(1)} %get-tuple-element.13.ent, f32[7,8,128]{2,1,0:T(8,128)S(1)} %get-tuple-element.14.ent_l, ...), custom_call_target="tpu_custom_call" | custom-call | tf_op jit(solution)/shard_map/transport/pallas_call | solution.py:564

commit v3 on v2

--- a/solution.py
+++ b/solution.py
@@ -12,6 +12,7 @@
 CAP = 0.2
 NV = 32
 CYCLES = 3
+CHUNK = 8
 SCALE = 1.0 / 512.0
 MESH = pl.DeviceIdType.MESH
 
@@ -269,7 +270,7 @@
 
 
 def conductance_setup(gath, w, ring, mats):
-    cond = [gath[pl.ds((v // 8) * 16 + v % 8, 8, stride=64), :] * SCALE for v in range(NV)]
+    cond = [gath[0, pl.ds(v, 8, stride=NV), :] * SCALE for v in range(NV)]
     level_weights(cond, 0, *w[0])
     c = coarsened(cond, 1)
     level_weights(c, 1, *w[1])
@@ -291,8 +292,7 @@
         return from_ring(x, sq, sq2, vecs.at[11])
 
     def body(_, carry):
-        at = [pl.ds((v // 8) * 16 + 8 + v % 8, 8, stride=64) for v in range(NV)]
-        source = [gath[s, :] * SCALE for s in at]
+        source = [gath[1, pl.ds(v, 8, stride=NV), :] * SCALE for v in range(NV)]
         x = vcycle(0, source, [pot[v] for v in range(NV)], w, coarse)
         for v in range(NV):
             pot[v] = x[v]
@@ -327,7 +327,7 @@
     ped, wind, cour, part, parts, gath, bsend, brecv, psend,
     wl0, ws0, wn0, kk0, dd0, wl1, ws1, wn1, kk1, wl2, ws2, wn2, kk2,
     sq, sq2, bmat, emat, ps, qs, gf, left, left2, pivots, vecs, pot, whole,
-    s_ld, s_t, r_t, s_l, r_l, s_h, r_h, s_b, r_b, s_p, r_p, s_e, r_e,
+    s_ld, s_t, r_t, s_l, r_l, s_h, r_h, s_b, r_b, s_p, r_p, s_e, r_e, line,
 ):
     ns, pts = dens.shape[:2]
     t, l = lax.axis_index("tube"), lax.axis_index("lon")
@@ -342,15 +342,15 @@
 
     far_t = sorted(range(1, nt), key=lambda o: -min(o, nt - o))
     far_l = sorted(range(1, nl), key=lambda o: -min(o // 2 % 4, 4 - o // 2 % 4) - min(o // 8, 4 - o // 8))
+    beside = l + 1 - 2 * lax.rem(l, 2)
+    x_line = [l - lax.rem(l, 8) + lax.rem(lax.rem(l, 8) + 2 * o, 8) for o in range(1, 4)]
+    y_line = [lax.rem(c + 8 * o, nl) for c in (l, beside) for o in range(1, nl // 8)]
+    next_chip = lax.rem(l + 2 * lax.rem(l, 2) - 1 + nl, nl)
+    across_lon = y_line + x_line + [beside, next_chip]
+    greeted = [(lax.rem(t + o, nt), l) for o in far_t] + [(t, c) for c in across_lon]
     barrier = pltpu.get_barrier_semaphore()
-    for o in far_t:
-        pl.semaphore_signal(
-            barrier, inc=1, device_id=(lax.rem(t + o, nt), l), device_id_type=MESH
-        )
-    for o in far_l:
-        pl.semaphore_signal(
-            barrier, inc=1, device_id=(t, lax.rem(l + o, nl)), device_id_type=MESH
-        )
+    for to in greeted:
+        pl.semaphore_signal(barrier, inc=1, device_id=to, device_id_type=MESH)
 
     loads[0].wait()
     loads[1].wait()
@@ -359,8 +359,8 @@
     for p in range(4, pts):
         csum[p % 4] = csum[p % 4] + ped[p]
         ssum[p % 4] = ssum[p % 4] + ped[p] * wind[p]
-    part[pl.ds(0, 8), :] = (csum[0] + csum[1]) + (csum[2] + csum[3])
-    part[pl.ds(8, 8), :] = (ssum[0] + ssum[1]) + (ssum[2] + ssum[3])
+    part[0] = (csum[0] + csum[1]) + (csum[2] + csum[3])
+    part[1] = (ssum[0] + ssum[1]) + (ssum[2] + ssum[3])
 
     def remote(src, dst, ssem, rsem, to):
         c = pltpu.make_async_remote_copy(
@@ -370,11 +370,14 @@
         c.start()
         return c
 
-    pl.semaphore_wait(barrier, nt + nl - 2)
+    pl.semaphore_wait(barrier, len(greeted))
+    for c in x_line:
+        pl.semaphore_signal(line, inc=1, device_id=(t, c), device_id_type=MESH)
     along = []
-    for o in far_t:
-        to = lax.rem(t + o, nt)
-        along.append(remote(part, parts.at[o], s_t.at[o], r_t.at[o], (to, l)))
+    for k in range(2):
+        for o in far_t:
+            to = (lax.rem(t + o, nt), l)
+            along.append(remote(part.at[k], parts.at[k, o], s_t.at[k, o], r_t.at[k, o], to))
 
     right, left_l = lax.rem(l + 1, nl), lax.rem(l + nl - 1, nl)
     h0 = remote(
@@ -412,18 +415,22 @@
             o = lax.rem(t - owner_of[s] + nt, nt)
             remote(bsend.at[s], brecv.at[o], s_b.at[s], r_b.at[o], (owner_of[s], l))
 
-    parts[0] = part[...]
-    total = None
-    for c in reversed(along):
-        c.wait_recv()
-    for o in range(nt):
-        total = parts[o] if total is None else total + parts[o]
-    gath[pl.ds(pl.multiple_of(l * 16, 16), 16), :] = total
-    mine_rows = gath.at[pl.ds(pl.multiple_of(l * 16, 16), 16), :]
     across = []
-    for o in far_l:
-        to = lax.rem(l + o, nl)
-        across.append(remote(mine_rows, mine_rows, s_l.at[o], r_l.at[o], (t, to)))
+    for k in range(2):
+        parts[k, 0] = part[k]
+        for c in along[k * (nt - 1) : (k + 1) * (nt - 1)]:
+            c.wait_recv()
+        total = [parts[k, o] for o in range(nt)]
+        while len(total) > 1:
+            total = [total[q] + total[q + 1] for q in range(0, len(total), 2)]
+        block = pl.ds(pl.multiple_of(l * 8, 8), 8)
+        gath[k, block, :] = total[0]
+        if k == 0:
+            pl.semaphore_wait(line, len(x_line))
+        for o in far_l:
+            to = (t, lax.rem(l + o, nl))
+            at = gath.at[k, block, :]
+            across.append(remote(at, at, s_l.at[k, o], r_l.at[k, o], to))
 
     @pl.when(is_owner)
     def _():
@@ -440,7 +447,7 @@
             to = lax.rem(t + o, nt)
             remote(psend.at[to], ent.at[mine], s_p.at[o], r_p.at[mine], (to, l))
 
-    for c in across:
+    for c in across[: nl - 1]:
         c.wait_recv()
 
     w = [(wl0, ws0, wn0, kk0, dd0), (wl1, ws1, wn1, kk1, None), (wl2, ws2, wn2, kk2, None)]
@@ -456,6 +463,8 @@
     e0 = remote(ent, ent_l, s_e.at[0], r_e.at[0], (t, right))
     e1 = remote(ent, ent_r, s_e.at[1], r_e.at[1], (t, left_l))
 
+    for c in across[nl - 1 :]:
+        c.wait_recv()
     cycles(gath, w, ring, mats, pot)
     for v in range(NV):
         whole[pl.ds(v, 8, stride=NV), :] = pot[v]
@@ -517,15 +526,16 @@
         out_specs=(VM,) * 9,
         scratch_shapes=[
             tiles(pts), tiles(pts), pltpu.VMEM((ns, pts), F32),
-            rows(16), pltpu.VMEM((nt, 16, 128), F32), rows(512),
+            tiles(2), tiles(2, nt), pltpu.VMEM((2, 8 * nl, 128), F32),
             tiles(ns, 2), tiles(nt, 2), tiles(nt),
         ]
         + levels
         + [rows(128), rows(128), rows(256), rows(256), rows(5 * 256), rows(5 * 256), rows(256)]
         + [rows(256), rows(256), rows(256), pltpu.VMEM((12, 16, 128), F32), tiles(NV), rows(256)]
         + [
-            dma((4,)), dma((nt,)), dma((nt,)), dma((nl,)), dma((nl,)), dma((2,)), dma((2,)),
+            dma((4,)), dma((2, nt)), dma((2, nt)), dma((2, nl)), dma((2, nl)), dma((2,)), dma((2,)),
             dma((ns,)), dma((nt,)), dma((nt,)), dma((ns,)), dma((2,)), dma((2,)),
+            pltpu.SemaphoreType.REGULAR,
         ],
         compiler_params=pltpu.CompilerParams(
             collective_id=0, has_side_effects=True, vmem_limit_bytes=40 * 2**20
@@ -534,7 +544,7 @@
     )(pedersen, wind, courant, density)
 
 
-def transport_kernel(coef, pot_in, ent, ent_l, ent_r, dens, halo, atab, btab, out, pot):
+def transport_kernel(coef, pot_in, ent, ent_l, ent_r, dens, halo, atab, btab, out_hbm, pot, out, sem):
     ns, pts = out.shape[:2]
     pot[...] = pot_in[...]
     cc, cw, ce, cs, cn = (coef[k] for k in range(5))
@@ -557,7 +567,14 @@
             new.append((y, side))
         return tuple(new)
 
-    lax.fori_loop(0, pts, step, tuple(start))
+    stores, carry = [], tuple(start)
+    for k in range(pts // CHUNK):
+        carry = lax.fori_loop(k * CHUNK, (k + 1) * CHUNK, step, carry, unroll=True)
+        at = pl.ds(k * CHUNK, CHUNK)
+        stores.append(pltpu.make_async_copy(out.at[:, at], out_hbm.at[:, at], sem.at[k]))
+        stores[-1].start()
+    for c in stores:
+        c.wait()
 
 
 def transport(coef, pot, ent, ent_l, ent_r, density, halo, atab, btab):
@@ -568,7 +585,8 @@
             jax.ShapeDtypeStruct((8, 128), F32),
         ),
         in_specs=[VM] * 9,
-        out_specs=(VM, VM),
+        out_specs=(pl.BlockSpec(memory_space=pl.ANY), VM),
+        scratch_shapes=[pltpu.VMEM(density.shape, F32), pltpu.SemaphoreType.DMA((density.shape[1] // CHUNK,))],
         compiler_params=pltpu.CompilerParams(vmem_limit_bytes=24 * 2**20),
         name="transport",
     )(coef, pot, ent, ent_l, ent_r, density, halo, atab, btab)

time: 49.2 us -> 44.6 us (0.907)
  Pallas kernels: 48.4 us -> 43.8 us
    pallas_call x1, Pallas kernels: 44.6 us -> 41.8 us  [dynamo(): pl.pallas_call(functools.partial(dynamo_kernel, nt, nl), out_shape=(jax.S...]
    pallas_call x1, Pallas kernels: 3.77 us -> 1.95 us  [transport(): pl.pallas_call(transport_kernel, out_shape=(jax.ShapeDtypeStruct(density....]
where the time goes in v3:
time: 44.6 us; the launch traced here: 44.4 us
  Pallas kernels  43.8 us (98%)
  between operations  0.64 us (1%)
    pallas_call x1, Pallas kernels, dynamo(): pl.pallas_call(functools.partial(dynamo_kernel, nt, nl), out_shape=(jax.S...  41.8 us
    pallas_call x1, Pallas kernels, transport(): pl.pallas_call(transport_kernel, out_shape=(jax.ShapeDtypeStruct(density....  1.95 us

profile of v3, /device:TPU:1, one launch (start us, length us, event | category | flops | bytes accessed | tf_op | source)
XLA Modules:
  0.0 44.4 jit_solution(9460543822072647362)
XLA Ops:
  0.6 41.8 %dynamo.1 = (f32[5,8,128]{2,1,0:T(8,128)S(1)}, f32[8,128]{1,0:T(8,128)S(1)}, f32[7,8,128]{2,1,0:T(8,128)S(1)}, f32[7,8,128]{2,1,0:T(8,128)S(1)}, f32[7,8,128]{2,...) custom-call(f32[32,8,128]{2,1,0:T(8,128)} %ped_hbm.1, ...), custom_call_target="tpu_custom_call" | custom-call | tf_op jit(solution)/shard_map/dynamo/pallas_call | solution.py:515
  42.5 1.9 %transport.1 = (f32[7,32,8,128]{3,2,1,0:T(8,128)}, f32[8,128]{1,0:T(8,128)}) custom-call(f32[5,8,128]{2,1,0:T(8,128)S(1)} %get-tuple-element.11.coef, f32[8,128]{1,0:T(8,128)S(1)} %get-tuple-element.12.pot_in, f32[7,8,128]{2,1,0:T(8,128)S(1)} %get-tuple-element.13.ent, f32[7,8,128]{2,1,0:T(8,128)S(1)} %get-tuple-element.14.ent_l, ...), custom_call_target="tpu_custom_call" | custom-call | tf_op jit(solution)/shard_map/transport/pallas_call | solution.py:581

commit v4 on v3

--- a/solution.py
+++ b/solution.py
@@ -12,6 +12,7 @@
 CAP = 0.2
 NV = 32
 CYCLES = 3
+SPLIT = 2
 CHUNK = 8
 SCALE = 1.0 / 512.0
 MESH = pl.DeviceIdType.MESH
@@ -269,18 +270,27 @@
     return times(gf, 0, vecs.at[10], r)
 
 
-def conductance_setup(gath, w, ring, mats):
+def coarse_setup(coarse, ring, mats):
+    sq, sq2, vecs = ring
+    bmat, emat, ps, qs, gf, left, left2, pivots = mats
+    lane = lax.broadcasted_iota(jnp.int32, (8, 128), 1)
+    for v in range(4):
+        y = coarse[pl.ds(v * 8, 8), :] * (SCALE / 64.0)
+        for step in (1, 2, 4):
+            y = y + jnp.where((lane // step) % 2 == 0, lroll(y, -step), lroll(y, step))
+        for rep in range(4):
+            sq[pl.ds(rep * 32 + v * 8, 8), :] = y
+    sq2[...] = sq[...].T
+    ring_matrix([sq2[pl.ds(64 * h, 8, stride=8), :] for h in range(2)], bmat, emat)
+    factor(bmat, emat, ps, qs, gf, left, left2, pivots)
+
+
+def conductance_setup(gath, w):
     cond = [gath[0, pl.ds(v, 8, stride=NV), :] * SCALE for v in range(NV)]
     level_weights(cond, 0, *w[0])
     c = coarsened(cond, 1)
     level_weights(c, 1, *w[1])
-    c = coarsened(c, 2)
-    level_weights(c, 2, *w[2])
-    c = coarsened(c, 4)
-    sq, sq2, vecs = ring
-    bmat, emat, ps, qs, gf, left, left2, pivots = mats
-    ring_matrix(to_ring(c, sq, sq2), bmat, emat)
-    factor(bmat, emat, ps, qs, gf, left, left2, pivots)
+    level_weights(coarsened(c, 2), 2, *w[2])
 
 
 def cycles(gath, w, ring, mats, pot):
@@ -291,16 +301,18 @@
         x = ring_solve(to_ring(r, sq, sq2), ps, qs, gf, vecs)
         return from_ring(x, sq, sq2, vecs.at[11])
 
-    def body(_, carry):
+    def sweep(start):
         source = [gath[1, pl.ds(v, 8, stride=NV), :] * SCALE for v in range(NV)]
-        x = vcycle(0, source, [pot[v] for v in range(NV)], w, coarse)
+        x = vcycle(0, source, start, w, coarse)
         for v in range(NV):
             pot[v] = x[v]
+
+    def body(_, carry):
+        sweep([pot[v] for v in range(NV)])
         return carry
 
-    for v in range(NV):
-        pot[v] = jnp.zeros((8, 128), F32)
-    lax.fori_loop(0, CYCLES, body, 0)
+    sweep(None)
+    lax.fori_loop(1, CYCLES, body, 0)
 
 
 def stencil(pot, west, east):
@@ -323,11 +335,11 @@
 
 def dynamo_kernel(
     nt, nl, ped_hbm, wind_hbm, cour_hbm, dens_hbm,
-    coef, pot_own, ent, ent_l, ent_r, dens, halo, atab, btab,
-    ped, wind, cour, part, parts, gath, bsend, brecv, psend,
+    coef, pot_own, ent, sides, dens, halo, atab, btab,
+    ped, wind, cour, part, parts, gath, crow, crows, coarse, rows32, bsend, brecv, psend,
     wl0, ws0, wn0, kk0, dd0, wl1, ws1, wn1, kk1, wl2, ws2, wn2, kk2,
     sq, sq2, bmat, emat, ps, qs, gf, left, left2, pivots, vecs, pot, whole,
-    s_ld, s_t, r_t, s_l, r_l, s_h, r_h, s_b, r_b, s_p, r_p, s_e, r_e, line,
+    s_ld, s_t, r_t, s_l, r_l, s_h, r_h, s_b, r_b, s_p, r_p, s_e, r_e, s_c, r_c, line,
 ):
     ns, pts = dens.shape[:2]
     t, l = lax.axis_index("tube"), lax.axis_index("lon")
@@ -359,7 +371,7 @@
     for p in range(4, pts):
         csum[p % 4] = csum[p % 4] + ped[p]
         ssum[p % 4] = ssum[p % 4] + ped[p] * wind[p]
-    part[0] = (csum[0] + csum[1]) + (csum[2] + csum[3])
+    part[0] = total = (csum[0] + csum[1]) + (csum[2] + csum[3])
     part[1] = (ssum[0] + ssum[1]) + (ssum[2] + ssum[3])
 
     def remote(src, dst, ssem, rsem, to):
@@ -370,14 +382,21 @@
         c.start()
         return c
 
+    def settle(ref, sem):
+        pltpu.make_async_copy(ref, ref, sem).wait()
+
     pl.semaphore_wait(barrier, len(greeted))
     for c in x_line:
         pl.semaphore_signal(line, inc=1, device_id=(t, c), device_id_type=MESH)
-    along = []
-    for k in range(2):
+    crow[...] = jnp.sum(total, axis=0, keepdims=True)
+    for o in far_t:
+        to = (lax.rem(t + o, nt), l)
+        remote(crow, crows.at[o], s_c.at[0], r_c.at[0], to)
+    fields = [pl.ds(k * (2 // SPLIT), 2 // SPLIT) for k in range(SPLIT)]
+    for k in range(SPLIT):
         for o in far_t:
             to = (lax.rem(t + o, nt), l)
-            along.append(remote(part.at[k], parts.at[k, o], s_t.at[k, o], r_t.at[k, o], to))
+            remote(part.at[fields[k]], parts.at[o, fields[k]], s_t.at[k], r_t.at[k], to)
 
     right, left_l = lax.rem(l + 1, nl), lax.rem(l + nl - 1, nl)
     h0 = remote(
@@ -413,58 +432,61 @@
         @pl.when(t != owner_of[s])
         def _():
             o = lax.rem(t - owner_of[s] + nt, nt)
-            remote(bsend.at[s], brecv.at[o], s_b.at[s], r_b.at[o], (owner_of[s], l))
-
-    across = []
-    for k in range(2):
-        parts[k, 0] = part[k]
-        for c in along[k * (nt - 1) : (k + 1) * (nt - 1)]:
-            c.wait_recv()
-        total = [parts[k, o] for o in range(nt)]
+            remote(bsend.at[s], brecv.at[o], s_b, r_b, (owner_of[s], l))
+
+    others_t, others_l = pl.ds(1, nt - 1), pl.ds(0, (nl - 1) * 8)
+    settle(crows.at[others_t], r_c.at[0])
+    total = [crow[...]] + [crows[o] for o in range(1, nt)]
+    while len(total) > 1:
+        total = [total[q] + total[q + 1] for q in range(0, len(total), 2)]
+    coarse[l] = total[0]
+    pl.semaphore_wait(line, len(x_line))
+    for o in far_l:
+        to = (t, lax.rem(l + o, nl))
+        remote(coarse.at[l], coarse.at[l], s_c.at[1], r_c.at[1], to)
+    block = pl.ds(pl.multiple_of(l * 8, 8), 8)
+    for k in range(SPLIT):
+        settle(parts.at[others_t, fields[k]], r_t.at[k])
+        total = [part[fields[k]]] + [parts[o, fields[k]] for o in range(1, nt)]
         while len(total) > 1:
             total = [total[q] + total[q + 1] for q in range(0, len(total), 2)]
-        block = pl.ds(pl.multiple_of(l * 8, 8), 8)
-        gath[k, block, :] = total[0]
-        if k == 0:
-            pl.semaphore_wait(line, len(x_line))
+        gath[fields[k], block, :] = total[0]
         for o in far_l:
             to = (t, lax.rem(l + o, nl))
-            at = gath.at[k, block, :]
-            across.append(remote(at, at, s_l.at[k, o], r_l.at[k, o], to))
+            at = gath.at[fields[k], block, :]
+            remote(at, at, s_l.at[k], r_l.at[k], to)
+
+    west_row, east_row = pl.ds(0, 1), pl.ds(7, 1)
 
     @pl.when(is_owner)
     def _():
         brecv[0] = bsend[mine]
-        for o in range(1, nt):
-            pltpu.make_async_copy(brecv.at[o], brecv.at[o], r_b.at[o]).wait()
+        settle(brecv.at[others_t], r_b)
         x = zero
         for k in range(nt):
             psend[k] = x
             o = lax.rem(k - t + nt, nt)
             x = brecv[o, 1] * x + brecv[o, 0]
         ent[mine] = psend[t]
-        for o in far_t:
+        for o in far_t + [0]:
             to = lax.rem(t + o, nt)
-            remote(psend.at[to], ent.at[mine], s_p.at[o], r_p.at[mine], (to, l))
-
-    for c in across[: nl - 1]:
-        c.wait_recv()
+            if o:
+                remote(psend.at[to], ent.at[mine], s_p, r_p, (to, l))
+            for k, (row, side) in enumerate(((east_row, right), (west_row, left_l))):
+                remote(psend.at[to, row], sides.at[mine, west_row if k == 0 else east_row],
+                       s_e, r_e, (to, side))
 
     w = [(wl0, ws0, wn0, kk0, dd0), (wl1, ws1, wn1, kk1, None), (wl2, ws2, wn2, kk2, None)]
     ring, mats = (sq, sq2, vecs), (bmat, emat, ps, qs, gf, left, left2, pivots)
-    conductance_setup(gath, w, ring, mats)
-
-    for s in range(ns):
-
-        @pl.when(t != owner_of[s])
-        def _():
-            pltpu.make_async_copy(ent.at[s], ent.at[s], r_p.at[s]).wait()
-
-    e0 = remote(ent, ent_l, s_e.at[0], r_e.at[0], (t, right))
-    e1 = remote(ent, ent_r, s_e.at[1], r_e.at[1], (t, left_l))
-
-    for c in across[nl - 1 :]:
-        c.wait_recv()
+    settle(coarse.at[pl.ds(0, nl - 1)], r_c.at[1])
+    for r in range(nl):
+        rows32[pl.ds(r, 1), :] = coarse[r]
+    coarse_setup(rows32, ring, mats)
+    settle(gath.at[fields[0], others_l], r_l.at[0])
+    conductance_setup(gath, w)
+
+    for k in range(1, SPLIT):
+        settle(gath.at[fields[k], others_l], r_l.at[k])
     cycles(gath, w, ring, mats, pot)
     for v in range(NV):
         whole[pl.ds(v, 8, stride=NV), :] = pot[v]
@@ -476,20 +498,26 @@
     for k, c in enumerate(stencil(own, west, east)):
         coef[k] = c
 
-    for c in along + across:
-        c.wait_send()
-    for s in range(ns):
-
-        @pl.when(t != owner_of[s])
-        def _():
-            pltpu.make_async_copy(bsend.at[s], bsend.at[s], s_b.at[s]).wait()
+    settle(crows.at[others_t], s_c.at[0])
+    settle(coarse.at[pl.ds(0, nl - 1)], s_c.at[1])
+    for k in range(SPLIT):
+        settle(parts.at[others_t, fields[k]], s_t.at[k])
+        settle(gath.at[fields[k], others_l], s_l.at[k])
 
     @pl.when(is_owner)
     def _():
-        for o in range(1, nt):
-            pltpu.make_async_copy(psend.at[0], psend.at[0], s_p.at[o]).wait()
-
-    for c in (h0, h1, e0, e1):
+        settle(bsend.at[pl.ds(0, ns - 1)], s_b)
+        settle(ent.at[pl.ds(0, ns - 1)], r_p)
+        settle(psend.at[others_t], s_p)
+        settle(psend.at[pl.ds(0, nt // 4)], s_e)
+
+    @pl.when(jnp.logical_not(is_owner))
+    def _():
+        settle(bsend, s_b)
+        settle(ent, r_p)
+
+    settle(sides.at[:, pl.ds(0, 2), :], r_e)
+    for c in (h0, h1):
         c.wait()
 
 
@@ -517,25 +545,25 @@
         out_shape=(
             jax.ShapeDtypeStruct((5, 8, 128), F32),
             jax.ShapeDtypeStruct((8, 128), F32),
-            state, state, state,
+            state, state,
             jax.ShapeDtypeStruct(density.shape, F32),
             jax.ShapeDtypeStruct(density.shape, F32),
             table, table,
         ),
         in_specs=[HBM] * 4,
-        out_specs=(VM,) * 9,
+        out_specs=(VM,) * 8,
         scratch_shapes=[
             tiles(pts), tiles(pts), pltpu.VMEM((ns, pts), F32),
-            tiles(2), tiles(2, nt), pltpu.VMEM((2, 8 * nl, 128), F32),
+            tiles(2), tiles(nt, 2), pltpu.VMEM((2, 8 * nl, 128), F32),
+            rows(1), pltpu.VMEM((nt, 1, 128), F32), pltpu.VMEM((nl, 1, 128), F32), rows(nl),
             tiles(ns, 2), tiles(nt, 2), tiles(nt),
         ]
         + levels
         + [rows(128), rows(128), rows(256), rows(256), rows(5 * 256), rows(5 * 256), rows(256)]
         + [rows(256), rows(256), rows(256), pltpu.VMEM((12, 16, 128), F32), tiles(NV), rows(256)]
         + [
-            dma((4,)), dma((2, nt)), dma((2, nt)), dma((2, nl)), dma((2, nl)), dma((2,)), dma((2,)),
-            dma((ns,)), dma((nt,)), dma((nt,)), dma((ns,)), dma((2,)), dma((2,)),
-            pltpu.SemaphoreType.REGULAR,
+            dma((4,)), dma((2,)), dma((2,)), dma((2,)), dma((2,)), dma((2,)), dma((2,)),
+            dma, dma, dma, dma, dma, dma, dma((2,)), dma((2,)), pltpu.SemaphoreType.REGULAR,
         ],
         compiler_params=pltpu.CompilerParams(
             collective_id=0, has_side_effects=True, vmem_limit_bytes=40 * 2**20
@@ -544,15 +572,12 @@
     )(pedersen, wind, courant, density)
 
 
-def transport_kernel(coef, pot_in, ent, ent_l, ent_r, dens, halo, atab, btab, out_hbm, pot, out, sem):
+def transport_kernel(coef, pot_in, ent, sides, dens, halo, atab, btab, out_hbm, pot, out, sem):
     ns, pts = out.shape[:2]
     pot[...] = pot_in[...]
     cc, cw, ce, cs, cn = (coef[k] for k in range(5))
     sub = lax.broadcasted_iota(jnp.int32, (8, 128), 0)
-    start = []
-    for s in range(ns):
-        side = jnp.where(sub == 0, pltpu.roll(ent_l[s], 1, 0), pltpu.roll(ent_r[s], 7, 0))
-        start.append((ent[s], side))
+    start = [(ent[s], sides[s]) for s in range(ns)]
 
     def step(p, carry):
         new = []
@@ -577,19 +602,19 @@
         c.wait()
 
 
-def transport(coef, pot, ent, ent_l, ent_r, density, halo, atab, btab):
+def transport(coef, pot, ent, sides, density, halo, atab, btab):
     return pl.pallas_call(
         transport_kernel,
         out_shape=(
             jax.ShapeDtypeStruct(density.shape, F32),
             jax.ShapeDtypeStruct((8, 128), F32),
         ),
-        in_specs=[VM] * 9,
+        in_specs=[VM] * 8,
         out_specs=(pl.BlockSpec(memory_space=pl.ANY), VM),
         scratch_shapes=[pltpu.VMEM(density.shape, F32), pltpu.SemaphoreType.DMA((density.shape[1] // CHUNK,))],
         compiler_params=pltpu.CompilerParams(vmem_limit_bytes=24 * 2**20),
         name="transport",
-    )(coef, pot, ent, ent_l, ent_r, density, halo, atab, btab)
+    )(coef, pot, ent, sides, density, halo, atab, btab)
 
 
 def solution(mesh):

time: 44.6 us -> 41.1 us (0.922)
  Pallas kernels: 43.8 us -> 40.4 us
    pallas_call x1, Pallas kernels: 41.8 us -> 38.4 us  [dynamo(): pl.pallas_call(functools.partial(dynamo_kernel, nt, nl), out_shape=(jax.S...]
where the time goes in v4:
time: 41.1 us; the launch traced here: 41 us
  Pallas kernels  40.4 us (98%)
  between operations  0.64 us (2%)
    pallas_call x1, Pallas kernels, dynamo(): pl.pallas_call(functools.partial(dynamo_kernel, nt, nl), out_shape=(jax.S...  38.4 us
    pallas_call x1, Pallas kernels, transport(): pl.pallas_call(transport_kernel, out_shape=(jax.ShapeDtypeStruct(density....  1.91 us

profile of v4, /device:TPU:1, one launch (start us, length us, event | category | flops | bytes accessed | tf_op | source)
XLA Modules:
  0.0 41.0 jit_solution(17978600546501799963)
XLA Ops:
  0.6 38.4 %dynamo.1 = (f32[5,8,128]{2,1,0:T(8,128)S(1)}, f32[8,128]{1,0:T(8,128)S(1)}, f32[7,8,128]{2,1,0:T(8,128)S(1)}, f32[7,8,128]{2,1,0:T(8,128)S(1)}, f32[7,32,8,128]...) custom-call(f32[32,8,128]{2,1,0:T(8,128)} %ped_hbm.1, ...), custom_call_target="tpu_custom_call" | custom-call | tf_op jit(solution)/shard_map/dynamo/pallas_call | solution.py:543
  39.1 1.9 %transport.1 = (f32[7,32,8,128]{3,2,1,0:T(8,128)}, f32[8,128]{1,0:T(8,128)}) custom-call(f32[5,8,128]{2,1,0:T(8,128)S(1)} %get-tuple-element.10.coef, f32[8,128]{1,0:T(8,128)S(1)} %get-tuple-element.11.pot_in, f32[7,8,128]{2,1,0:T(8,128)S(1)} %get-tuple-element.12.ent, f32[7,8,128]{2,1,0:T(8,128)S(1)} %get-tuple-element.13.sides, ...), custom_call_target="tpu_custom_call" | custom-call | tf_op jit(solution)/shard_map/transport/pallas_call | solution.py:606

commit v5 on v4

--- a/solution.py
+++ b/solution.py
@@ -359,20 +359,20 @@
     y_line = [lax.rem(c + 8 * o, nl) for c in (l, beside) for o in range(1, nl // 8)]
     next_chip = lax.rem(l + 2 * lax.rem(l, 2) - 1 + nl, nl)
     across_lon = y_line + x_line + [beside, next_chip]
-    greeted = [(lax.rem(t + o, nt), l) for o in far_t] + [(t, c) for c in across_lon]
+    greeted = [(t, c) for c in across_lon] + [(lax.rem(t + o, nt), l) for o in far_t]
     barrier = pltpu.get_barrier_semaphore()
     for to in greeted:
         pl.semaphore_signal(barrier, inc=1, device_id=to, device_id_type=MESH)
 
+    def summed(terms):
+        terms = list(terms)
+        while len(terms) > 1:
+            terms = [x + y for x, y in zip(terms[::2], terms[1::2])] + terms[len(terms) & ~1 :]
+        return terms[0]
+
     loads[0].wait()
-    loads[1].wait()
-    csum = [ped[k] for k in range(4)]
-    ssum = [ped[k] * wind[k] for k in range(4)]
-    for p in range(4, pts):
-        csum[p % 4] = csum[p % 4] + ped[p]
-        ssum[p % 4] = ssum[p % 4] + ped[p] * wind[p]
-    part[0] = total = (csum[0] + csum[1]) + (csum[2] + csum[3])
-    part[1] = (ssum[0] + ssum[1]) + (ssum[2] + ssum[3])
+    part[0] = total = summed(ped[p] for p in range(pts))
+    crow[...] = jnp.sum(total, axis=0, keepdims=True)
 
     def remote(src, dst, ssem, rsem, to):
         c = pltpu.make_async_remote_copy(
@@ -386,14 +386,16 @@
         pltpu.make_async_copy(ref, ref, sem).wait()
 
     pl.semaphore_wait(barrier, len(greeted))
-    for c in x_line:
-        pl.semaphore_signal(line, inc=1, device_id=(t, c), device_id_type=MESH)
-    crow[...] = jnp.sum(total, axis=0, keepdims=True)
     for o in far_t:
         to = (lax.rem(t + o, nt), l)
         remote(crow, crows.at[o], s_c.at[0], r_c.at[0], to)
+    for c in x_line:
+        pl.semaphore_signal(line, inc=1, device_id=(t, c), device_id_type=MESH)
     fields = [pl.ds(k * (2 // SPLIT), 2 // SPLIT) for k in range(SPLIT)]
     for k in range(SPLIT):
+        if k == SPLIT - 1:
+            loads[1].wait()
+            part[1] = summed(ped[p] * wind[p] for p in range(pts))
         for o in far_t:
             to = (lax.rem(t + o, nt), l)
             remote(part.at[fields[k]], parts.at[o, fields[k]], s_t.at[k], r_t.at[k], to)
@@ -478,6 +480,11 @@
 
     w = [(wl0, ws0, wn0, kk0, dd0), (wl1, ws1, wn1, kk1, None), (wl2, ws2, wn2, kk2, None)]
     ring, mats = (sq, sq2, vecs), (bmat, emat, ps, qs, gf, left, left2, pivots)
+    settle(crows.at[others_t], s_c.at[0])
+    for k in range(SPLIT):
+        settle(parts.at[others_t, fields[k]], s_t.at[k])
+    for c in (h0, h1):
+        c.wait()
     settle(coarse.at[pl.ds(0, nl - 1)], r_c.at[1])
     for r in range(nl):
         rows32[pl.ds(r, 1), :] = coarse[r]
@@ -498,10 +505,8 @@
     for k, c in enumerate(stencil(own, west, east)):
         coef[k] = c
 
-    settle(crows.at[others_t], s_c.at[0])
     settle(coarse.at[pl.ds(0, nl - 1)], s_c.at[1])
     for k in range(SPLIT):
-        settle(parts.at[others_t, fields[k]], s_t.at[k])
         settle(gath.at[fields[k], others_l], s_l.at[k])
 
     @pl.when(is_owner)
@@ -517,8 +522,6 @@
         settle(ent, r_p)
 
     settle(sides.at[:, pl.ds(0, 2), :], r_e)
-    for c in (h0, h1):
-        c.wait()
 
 
 VM = pl.BlockSpec(memory_space=pltpu.VMEM)

time: 41.1 us -> 40.9 us (level)
  no operation moved by 1% of the time
where the time goes in v5:
time: 40.9 us; the launch traced here: 40.8 us
  Pallas kernels  40.1 us (98%)
  between operations  0.64 us (2%)
    pallas_call x1, Pallas kernels, dynamo(): pl.pallas_call(functools.partial(dynamo_kernel, nt, nl), out_shape=(jax.S...  38.2 us
    pallas_call x1, Pallas kernels, transport(): pl.pallas_call(transport_kernel, out_shape=(jax.ShapeDtypeStruct(density....  1.91 us

profile of v5, /device:TPU:1, one launch (start us, length us, event | category | flops | bytes accessed | tf_op | source)
XLA Modules:
  0.0 40.8 jit_solution(7113511985563691010)
XLA Ops:
  0.6 38.2 %dynamo.1 = (f32[5,8,128]{2,1,0:T(8,128)S(1)}, f32[8,128]{1,0:T(8,128)S(1)}, f32[7,8,128]{2,1,0:T(8,128)S(1)}, f32[7,8,128]{2,1,0:T(8,128)S(1)}, f32[7,32,8,128]...) custom-call(f32[32,8,128]{2,1,0:T(8,128)} %ped_hbm.1, ...), custom_call_target="tpu_custom_call" | custom-call | tf_op jit(solution)/shard_map/dynamo/pallas_call | solution.py:546
  38.9 1.9 %transport.1 = (f32[7,32,8,128]{3,2,1,0:T(8,128)}, f32[8,128]{1,0:T(8,128)}) custom-call(f32[5,8,128]{2,1,0:T(8,128)S(1)} %get-tuple-element.10.coef, f32[8,128]{1,0:T(8,128)S(1)} %get-tuple-element.11.pot_in, f32[7,8,128]{2,1,0:T(8,128)S(1)} %get-tuple-element.12.ent, f32[7,8,128]{2,1,0:T(8,128)S(1)} %get-tuple-element.13.sides, ...), custom_call_target="tpu_custom_call" | custom-call | tf_op jit(solution)/shard_map/transport/pallas_call | solution.py:609
